TPU v7x, 128 devices: a whole 4x4x4 slice. The times are simulated.
128 devices in a mesh: kpair: 32 (over z, x, core), vir: 4 (over y).
Axes of the slice: x: 4, y: 4, z: 4, core: 2. Of those that a mesh axis runs over, the one named last changes fastest.
Arguments:
- lam: bfloat16 [32, 256, 9216], P('kpair', None, 'vir'), may hold values from -6 to 6
- chol: bfloat16 [32, 384, 9216], P('kpair', None, 'vir'), may hold values from -0.3125 to 0.3125
- cycle_int: bfloat16 [32, 1536, 1536], P('kpair', 'vir'), may hold values from -0.15625 to 0.15625
- sources: int32 [32, 2], replicated, may hold values from 0 to 31, as said below
Outputs:
- resid: float32 [32, 256, 9216], P('kpair', None, 'vir')
Inputs may be any that keep to these rules, and one draw needn't show every extreme that they name: `sources`: column 0 is a permutation of the 32 blocks; column 1 names any block, and several targets may name the same one; both columns reach 0 and 31.
All inputs are finite; a program needn't handle non-finite values.
Results may differ from a plain program's by a relative error of at most 0.0026.
Values may be sent and summed in bfloat16 or wider, within the bound.
A program may use at most 192 MiB of HBM per device.

v0:
```python
import math

import jax
import jax.numpy as jnp
from jax import lax
from jax.sharding import PartitionSpec as P

O = 16
V = 96


def local(lam, chol, cycle_int, sources):
    count = lax.axis_size("kpair")
    own = lam[0]
    rows_all = own.shape[0]
    width = own.shape[1]
    piece = rows_all // count
    spread = lax.all_to_all(
        own.reshape(count, piece, width), "kpair", split_axis=0, concat_axis=0, tiled=True
    )
    chosen = spread[jnp.transpose(sources)]
    back = lax.all_to_all(chosen, "kpair", split_axis=1, concat_axis=1, tiled=True)
    picked = back.reshape(2, rows_all, width)
    ladder_src = picked[0]
    cycle_src = picked[1]
    factor_local = chol[0]
    naux = factor_local.shape[0]
    slab = factor_local.shape[1] // V
    factor_full = lax.all_gather(factor_local, "vir", axis=1, tiled=True).reshape(naux, V, V)
    factor_flip = jnp.transpose(factor_full, (0, 2, 1)).reshape(naux, V * V)
    factor_part = factor_local.reshape(naux, slab, V)
    ladder_full = lax.all_gather(ladder_src, "vir", axis=1, tiled=True)
    a_block = math.gcd(slab, 8)

    def step(turn, total):
        start = turn * a_block
        part = lax.dynamic_slice_in_dim(factor_part, start, a_block, 1).reshape(naux, a_block * V)
        block = lax.dot_general(
            part, factor_flip, (((0,), (0,)), ((), ())), preferred_element_type=jnp.float32
        )
        block = block.astype(jnp.bfloat16).reshape(a_block, V * V, V)
        out = lax.dot_general(
            ladder_full, block, (((1,), (1,)), ((), ())), preferred_element_type=jnp.float32
        )
        return lax.dynamic_update_slice_in_dim(total, out, start, 1)

    ladder = lax.fori_loop(0, slab // a_block, step, jnp.zeros((rows_all, slab, V), jnp.float32))
    ladder = ladder.reshape(rows_all, slab * V)
    right_full = lax.all_gather(cycle_int[0], "vir", axis=0, tiled=True)
    right = right_full.reshape(V, O, O, V)
    left = cycle_src.reshape(O, O, slab, V)
    cycle = jnp.einsum("ikac,ckjb->ijab", left, right, preferred_element_type=jnp.float32)
    cycle = cycle.reshape(rows_all, slab * V)
    return (ladder + cycle)[None]


def solution(mesh):
    placed = (P("kpair", None, "vir"), P("kpair", None, "vir"), P("kpair", "vir", None), P())
    return jax.shard_map(
        local, mesh=mesh, in_specs=placed, out_specs=P("kpair", None, "vir"), check_vma=False
    )
```

profile of v0, /device:TPU:1, one launch (start us, length us, event | category | flops | bytes accessed | tf_op | source)
XLA Modules:
  0.0 374.8 jit_solution(15743280565246201031)
XLA Ops:
  6.5 0.0 all-gather.10.cloned.1.call-start
  6.5 0.7 all-gather.10.cloned.1.call-update
  7.3 0.0 all-gather.8.cloned.1.call-start
  7.3 3.9 %copy.25 = bf16[1,384,2304]{1,2,0:T(8,128)(2,1)} copy(bf16[1,384,2304]{2,1,0:T(8,128)(2,1)} %param.7) | data formatting | bytes 3538944 | tf_op args[1]
  11.2 0.0 copy-start
  11.2 0.0 all-gather.8.cloned.1.call-update
  11.2 9.4 %all-to-all-start = ((bf16[32,8,2304]{2,1,0:T(8,128)(2,1)}), bf16[32,8,2304]{2,1,0:T(8,128)(2,1)S(1)}, u32[]{:S(2)}, u32[]{:S(2)}) async-start(bf16[32,8,2304]{2,1,0:T(8,128)(2,1)} %bitcast.7), calls=%async_computation | async-start | bytes 2359296 | tf_op jit(solution)/shard_map/all_to_all | solution.py:18
  20.7 0.0 all-gather.6.cloned.1.call-start
  20.7 0.0 copy-done
  20.7 0.1 reshape.58
  20.8 17.5 %all-to-all-done = bf16[32,8,2304]{2,1,0:T(8,128)(2,1)S(1)} async-done(((bf16[32,8,2304]{2,1,0:T(8,128)(2,1)}), bf16[32,8,2304]{2,1,0:T(8,128)(2,1)S(1)}, u32[]{:S(2)}, u32[]{:S(2)}) %all-to-all-start) | async-done | bytes 1179680 | tf_op jit(solution)/shard_map/all_to_all | solution.py:18
  38.3 0.7 gather_fusion
  39.1 0.2 copy.28
  39.2 35.9 %all_to_all.10 = bf16[2,32,8,2304]{3,2,0,1:T(8,128)(2,1)S(1)} all-to-all(bf16[2,32,8,2304]{3,2,0,1:T(8,128)(2,1)S(1)} %copy.28), channel_id=1, replica_groups=mesh['kpair'=32,'vir'=4] {'kpair'}, dimensions={1} | all-to-all | bytes 4718592 | tf_op jit(solution)/shard_map/all_to_all | solution.py:22
  75.1 1.2 slice_bitcast_fusion
  76.2 0.0 all-gather.6.cloned.1.call-update
  76.3 3.3 reshape.71
  79.6 0.0 all-gather.10.cloned.1.call-done
  79.6 10.6 %reshape.54 = bf16[96,16,16,96]{3,2,1,0:T(8,128)(2,1)} reshape(bf16[1,1536,1536]{2,1,0:T(8,128)(2,1)} %all-gather.10.cloned.1.call-done) | data formatting | bytes 9437184 | tf_op jit(solution)/shard_map/reshape | solution.py:50
  90.2 8.6 %fusion.11 = f32[16,16,24,96]{3,2,1,0:T(8,128)S(1)} fusion(bf16[96,16,16,96]{3,2,1,0:T(8,128)(2,1)} %reshape.54, bf16[16,16,24,96,1]{3,2,1,0,4:T(8,128)(2,1)} %reshape.71), kind=kOutput, calls=%fused_computation.11 | convolution fusion | flops 1811939328 | bytes 8257536 | tf_op jit(solution)/shard_map/ikac,ckjb->ijab/dot_general | solution.py:52
  98.8 2.0 reshape.55
  100.8 2.0 copy.31
  102.9 36.3 %all-gather.8.cloned.1.call-done = bf16[1,384,9216]{1,2,0:T(8,128)(2,1)} async-done(((bf16[1,384,2304]{1,2,0:T(8,128)(2,1)}), bf16[1,384,9216]{1,2,0:T(8,128)(2,1)}) %all-gather.8.cloned.1.call-update) | async-done | bytes 7077904 | tf_op jit(solution)/shard_map/all_gather | solution.py:29
  139.2 8.5 %copy.27 = bf16[384,96,96]{0,2,1:T(8,128)(2,1)} copy(bf16[384,96,96]{0,1,2:T(8,128)(2,1)} %bitcast.63) | data formatting | bytes 14155776 | tf_op jit(solution)/shard_map/transpose | solution.py:30
  147.8 10.3 %copy.29 = bf16[384,9216]{1,0:T(8,128)(2,1)} copy(bf16[384,9216]{0,1:T(8,128)(2,1)} %bitcast.59) | data formatting | bytes 14155776 | tf_op jit(solution)/shard_map/while | solution.py:47
  158.1 36.2 %all-gather.6.cloned.1.call-done = bf16[256,9216]{1,0:T(8,128)(2,1)} async-done(((bf16[256,2304]{1,0:T(8,128)(2,1)}), bf16[256,9216]{1,0:T(8,128)(2,1)}) %all-gather.6.cloned.1.call-update) | async-done | bytes 4718608 | tf_op jit(solution)/shard_map/all_gather | solution.py:32
  194.3 1.7 broadcast_in_dim.7
  196.0 165.9 %while.13 = (s32[]{:T(128)}, f32[256,24,96]{0,2,1:T(8,128)}, bf16[384,24,96]{0,2,1:T(8,128)(2,1)}, bf16[384,9216]{1,0:T(8,128)(2,1)}, bf16[256,9216]{1,0:T(8,128...) while((s32[]{:T(128)}, f32[256,24,96]{0,2,1:T(8,128)}, bf16[384,24,96]{0,2,1:T(8,128)(2,1)}, ...), condition=%wide.region_1.0_spmd, body=%wide.region_0.0_spmd.sunk | while | flops 9066774528 | bytes 75694224 | solution.py:47
  196.0 1.1 constant_dynamic-slice_fusion.2
  197.1 13.2 %convolution_convert_fusion.2 = bf16[768,9216]{1,0:T(8,128)(2,1)} fusion(bf16[384,768]{0,1:T(8,128)(2,1)S(1)} %bitcast.61, bf16[384,9216]{1,0:T(8,128)(2,1)} %get-tuple-element.179), kind=kOutput, calls=%fused_computation.1.clone.1 | convolution fusion | flops 5442895872 | bytes 21823488 | tf_op jit(solution)/shard_map/while/body/eval_jaxpr/dot_general | solution.py:38
  210.3 27.3 %reshape.76 = bf16[8,9216,96]{2,1,0:T(8,128)(2,1)} reshape(bf16[768,9216]{1,0:T(8,128)(2,1)} %convolution_convert_fusion.2) | data formatting | bytes 28311552 | tf_op jit(solution)/shard_map/while/body/eval_jaxpr/reshape | solution.py:41
  237.6 13.7 %fusion.27 = f32[256,24,96]{0,2,1:T(8,128)} fusion(f32[256,24,96]{0,2,1:T(8,128)} %get-tuple-element.168, s32[]{:T(128)S(6)} %select_n.14, bf16[8,9216,96]{2,1,0:T(8,128)(2,1)} %reshape.76, bf16[256,9216]{1,0:T(8,128)(2,1)} %get-tuple-element.180), kind=kOutput, calls=%fused_computation.5.clone.1 | convolution fusion | flops 3623878656 | bytes 24379396 | tf_op jit(solution)/shard_map/while/body/eval_jaxpr/dot_general | solution.py:42
  251.3 1.1 constant_dynamic-slice_fusion.2
  252.4 13.2 %convolution_convert_fusion.2 = bf16[768,9216]{1,0:T(8,128)(2,1)} fusion(bf16[384,768]{0,1:T(8,128)(2,1)S(1)} %bitcast.61, bf16[384,9216]{1,0:T(8,128)(2,1)} %get-tuple-element.179), kind=kOutput, calls=%fused_computation.1.clone.1 | convolution fusion | flops 5442895872 | bytes 21823488 | tf_op jit(solution)/shard_map/while/body/eval_jaxpr/dot_general | solution.py:38
  265.6 27.3 %reshape.76 = bf16[8,9216,96]{2,1,0:T(8,128)(2,1)} reshape(bf16[768,9216]{1,0:T(8,128)(2,1)} %convolution_convert_fusion.2) | data formatting | bytes 28311552 | tf_op jit(solution)/shard_map/while/body/eval_jaxpr/reshape | solution.py:41
  292.9 13.7 %fusion.27 = f32[256,24,96]{0,2,1:T(8,128)} fusion(f32[256,24,96]{0,2,1:T(8,128)} %get-tuple-element.168, s32[]{:T(128)S(6)} %select_n.14, bf16[8,9216,96]{2,1,0:T(8,128)(2,1)} %reshape.76, bf16[256,9216]{1,0:T(8,128)(2,1)} %get-tuple-element.180), kind=kOutput, calls=%fused_computation.5.clone.1 | convolution fusion | flops 3623878656 | bytes 24379396 | tf_op jit(solution)/shard_map/while/body/eval_jaxpr/dot_general | solution.py:42
  306.5 1.1 constant_dynamic-slice_fusion.2
  307.7 13.2 %convolution_convert_fusion.2 = bf16[768,9216]{1,0:T(8,128)(2,1)} fusion(bf16[384,768]{0,1:T(8,128)(2,1)S(1)} %bitcast.61, bf16[384,9216]{1,0:T(8,128)(2,1)} %get-tuple-element.179), kind=kOutput, calls=%fused_computation.1.clone.1 | convolution fusion | flops 5442895872 | bytes 21823488 | tf_op jit(solution)/shard_map/while/body/eval_jaxpr/dot_general | solution.py:38
  320.9 27.3 %reshape.76 = bf16[8,9216,96]{2,1,0:T(8,128)(2,1)} reshape(bf16[768,9216]{1,0:T(8,128)(2,1)} %convolution_convert_fusion.2) | data formatting | bytes 28311552 | tf_op jit(solution)/shard_map/while/body/eval_jaxpr/reshape | solution.py:41
  348.1 13.7 %fusion.27 = f32[256,24,96]{0,2,1:T(8,128)} fusion(f32[256,24,96]{0,2,1:T(8,128)} %get-tuple-element.168, s32[]{:T(128)S(6)} %select_n.14, bf16[8,9216,96]{2,1,0:T(8,128)(2,1)} %reshape.76, bf16[256,9216]{1,0:T(8,128)(2,1)} %get-tuple-element.180), kind=kOutput, calls=%fused_computation.5.clone.1 | convolution fusion | flops 3623878656 | bytes 24379396 | tf_op jit(solution)/shard_map/while/body/eval_jaxpr/dot_general | solution.py:42
  361.8 3.4 bitcast_add_fusion
  365.2 3.0 copy.32
  (2 shorter events, 0.0 us)
Async XLA Ops:
  6.5 73.0 %all-gather.10.cloned.1.call-start = ((), (), s32[]{:S(2)}) async-start(), calls=%async_computation.4 | async-start | bytes 5898240 | tf_op jit(solution)/shard_map/all_gather | solution.py:49
  7.3 132.0 %all-gather.8.cloned.1.call-start = ((), (), s32[]{:S(2)}) async-start(), calls=%async_computation.3 | async-start | bytes 8847360 | tf_op jit(solution)/shard_map/all_gather | solution.py:29
  11.2 9.5 %copy-start = (s32[32,2]{0,1:T(2,128)S(1)}, s32[32,2]{0,1:T(2,128)}, u32[]{:S(2)}) copy-start(s32[32,2]{0,1:T(2,128)} %param.9) | copy-start | bytes 772
  11.2 27.1 %all-to-all-start = ((bf16[32,8,2304]{2,1,0:T(8,128)(2,1)}), bf16[32,8,2304]{2,1,0:T(8,128)(2,1)S(1)}, u32[]{:S(2)}, u32[]{:S(2)}) async-start(bf16[32,8,2304]{2,1,0:T(8,128)(2,1)} %bitcast.7), calls=%async_computation | async-start | bytes 2359296 | tf_op jit(solution)/shard_map/all_to_all | solution.py:18
  20.7 173.6 %all-gather.6.cloned.1.call-start = ((), (), s32[]{:S(2)}) async-start(), calls=%async_computation.2 | async-start | bytes 5898240 | tf_op jit(solution)/shard_map/all_gather | solution.py:32
Sparse Core Ops, SparseCore 0:
  9.0 55.8 all-gather.9
  66.6 72.6 all-gather.7
  140.9 53.3 all-gather.5
where the time goes:
time: 378 us; the launch traced here: 375 us
  local copies, waits for them, and re-layouts  133 us (35%)
  waiting for transfers between devices  90.8 us (24%)
  matrix products  89.2 us (24%)
  blocking collectives  35.9 us (9%)
  between operations  13.2 us (3%)
  starting transfers between devices  9.53 us (3%)
    reshape x3, local copies, waits for them, and re-layouts, step(): block = block.astype(jnp.bfloat16).reshape(a_block, V * V, V)  81.8 us
    dot_general x3, matrix products, step(): lax.dot_general(ladder_full, block, (((1,), (1,)), ((), ())), preferred_e...  41 us
    dot_general x3, matrix products, step(): lax.dot_general(part, factor_flip, (((0,), (0,)), ((), ())), preferred_el...  39.6 us
    all_gather x1, waiting for transfers between devices, local(): lax.all_gather(factor_local, 'vir', axis=1, tiled=True).reshape(naux, V, V)  36.3 us
    all_gather x1, waiting for transfers between devices, local(): ladder_full = lax.all_gather(ladder_src, 'vir', axis=1, tiled=True)  36.2 us
    all_to_all x1, blocking collectives, local(): lax.all_to_all(chosen, 'kpair', split_axis=1, concat_axis=1, tiled=True)  35.9 us
    all_to_all x1, waiting for transfers between devices, local(): lax.all_to_all(own.reshape(count, piece, width), 'kpair', split_axis=0, c...  17.5 us
    reshape x1, local copies, waits for them, and re-layouts, local(): right = right_full.reshape(V, O, O, V)  10.6 us
  transfers between devices with their start and end apart: 4, of which 3 were waited for; matrix products, arithmetic and copies ran while one was open for 14% of the time, Pallas kernels for 0%

commit v1 on v0

v1 whole, which is shorter than its diff:
```python
import functools

import jax
import jax.numpy as jnp
from jax import lax
from jax.experimental import pallas as pl
from jax.experimental.pallas import tpu as pltpu
from jax.sharding import PartitionSpec as P

O = 16
V = 96
VS = 24
NAUX = 384
OO = O * O
SLAB = VS * V
PAD = 128
BF = jnp.bfloat16
F32 = jnp.float32
MESH = pl.DeviceIdType.MESH
B_CHUNKS = 4


class Place:
    def __init__(self):
        kp = lax.axis_index("kpair")
        y = lax.axis_index("vir")
        core = kp % 2
        half = y // 2
        guest = (core + half) % 2
        other = y + 1 - 2 * (y % 2)
        swap = kp + 1 - 2 * core
        self.kp, self.y, self.half, self.guest = kp, y, half, guest
        self.home = guest == 0
        self.away = guest == 1
        self.mate = (swap, y)
        self.cross = (kp, other)
        self.partner = (swap, 3 - y)
        self.own_slab = y + guest * (3 - 2 * y)
        self.mate_slab = y + (1 - guest) * (3 - 2 * y)
        self.cross_slab = other + guest * (3 - 2 * other)
        self.diag_slab = other + (1 - guest) * (3 - 2 * other)


def remote(src, dst, send, recv, device):
    return pltpu.make_async_remote_copy(
        src_ref=src, dst_ref=dst, send_sem=send, recv_sem=recv, device_id=device, device_id_type=MESH
    )


def loop(count, body):
    def step(i, carry):
        body(i)
        return carry

    lax.fori_loop(0, count, step, 0)


def rows_of(index, size):
    return pl.ds(pl.multiple_of(index * size, size), size)


def spread_kernel(
    n, src, lam, ft, pt, lw, sw, fall, ptw, z, stage, z_send, z_recv, w_send, w_recv, b_send, b_recv, p_send, p_recv, own_sem
):
    at = Place()
    rows = 2 * OO // n
    lanes = SLAB // 2

    def piece(ref, q):
        return ref.at[rows_of(q // 2, rows), pl.ds(pl.multiple_of((q % 2) * lanes, 128), lanes)]

    barrier = pltpu.get_barrier_semaphore()

    def greet(o):
        pl.semaphore_signal(barrier, inc=1, device_id=((at.kp + o) % n, 3 - at.y), device_id_type=MESH)

    def greet_plane(o):
        pl.semaphore_signal(barrier, inc=1, device_id=((at.kp + o + 1) % n, at.y), device_id_type=MESH)

    pl.semaphore_signal(barrier, inc=1, device_id=at.cross, device_id_type=MESH)
    loop(n, greet)
    loop(n - 1, greet_plane)
    pl.semaphore_wait(barrier, 2 * n)

    def spread(o):
        q = (at.kp + o + 1) % n
        return remote(piece(lam, q), z.at[at.kp], z_send.at[q], z_recv.at[at.kp], (q, at.y))

    def spread_in(o):
        q = (at.kp + o + 1) % n
        return remote(piece(lam, at.kp), z.at[q], z_send.at[q], z_recv.at[q], (q, at.y))

    z_own = pltpu.make_async_copy(piece(lam, at.kp), z.at[at.kp], z_recv.at[at.kp])
    loop(n - 1, lambda o: spread(o).start())
    z_own.start()

    step = SLAB // B_CHUNKS

    def chunk(ref, k):
        return ref.at[pl.ds(k * step, step)]

    def b_copy(kind, src_ref, slab, k, device):
        return remote(chunk(src_ref, k), chunk(fall.at[slab], k), b_send.at[kind, k], b_recv.at[kind, k], device)

    f_own = pltpu.make_async_copy(ft, fall.at[at.own_slab], own_sem.at[0])
    p_own = pltpu.make_async_copy(pt, ptw, own_sem.at[1])
    p_swap = remote(pt, ptw, p_send, p_recv, at.partner)

    @pl.when(at.home)
    def _():
        for k in range(B_CHUNKS):
            b_copy(1, ft, at.own_slab, k, at.cross).start()
            b_copy(0, ft, at.own_slab, k, at.mate).start()
        f_own.start()
        p_own.start()

    @pl.when(at.away)
    def _():
        for k in range(B_CHUNKS):
            b_copy(3, ft, at.y, k, at.partner).start()
        p_swap.start()

    def relay(ks):
        @pl.when(at.away)
        def _():
            for k in ks:
                b_copy(3, ft, at.own_slab, k, at.partner).wait_recv()
                b_copy(1, fall.at[at.own_slab], at.own_slab, k, at.cross).start()
                b_copy(0, fall.at[at.own_slab], at.own_slab, k, at.mate).start()

    def forward(ks):
        for k in ks:
            b_copy(1, ft, at.cross_slab, k, at.cross).wait_recv()
            b_copy(2, fall.at[at.cross_slab], at.cross_slab, k, at.mate).start()

    def place(kind, t, q):
        e = t % 2
        moved = (e + at.half) % 2
        device = (t + moved * (1 - 2 * e), at.y + moved * (3 - 2 * at.y))
        out = lw if kind == 0 else sw
        return remote(stage.at[kind, t], piece(out, at.kp), w_send.at[kind, t], w_recv.at[kind, at.kp], device)

    def place_own(kind):
        out = lw if kind == 0 else sw
        return pltpu.make_async_copy(stage.at[kind, at.kp], piece(out, at.kp), w_recv.at[kind, at.kp])

    def place_in(kind, q):
        out = lw if kind == 0 else sw
        return remote(stage.at[kind, q], piece(out, q), w_send.at[kind, q], w_recv.at[kind, q], at.partner)

    def send_picked(kind):
        def pick(t):
            stage[kind, t] = z[src[t, kind]]

        def send(o):
            t = (at.kp + o + 1) % n
            place(kind, t, 0).start()

        loop(n, pick)
        loop(n - 1, send)

        @pl.when(at.home)
        def _():
            place_own(kind).start()

        @pl.when(at.away)
        def _():
            place(kind, at.kp, 0).start()

    relay(range(0, B_CHUNKS // 2))
    loop(n - 1, lambda o: spread_in(o).wait_recv())
    z_own.wait()
    send_picked(0)
    send_picked(1)
    relay(range(B_CHUNKS // 2, B_CHUNKS))
    forward(range(B_CHUNKS))

    for kind in (0, 1):

        @pl.when(at.home)
        def _():
            loop(n - 1, lambda o: place_in(kind, (at.kp + o + 1) % n).wait_recv())
            place_own(kind).wait()

        @pl.when(at.away)
        def _():
            loop(n, lambda q: place_in(kind, q).wait_recv())

    for k in range(B_CHUNKS):
        b_copy(0, ft, at.mate_slab, k, at.mate).wait_recv()
        b_copy(2, ft, at.diag_slab, k, at.mate).wait_recv()

    loop(n - 1, lambda o: spread(o).wait_send())
    for kind in (0, 1):
        loop(n - 1, lambda o: place(kind, (at.kp + o + 1) % n, 0).wait_send())

    @pl.when(at.home)
    def _():
        f_own.wait()
        p_own.wait()

    @pl.when(at.away)
    def _():
        for kind in (0, 1):
            place(kind, at.kp, 0).wait_send()
        for k in range(B_CHUNKS):
            b_copy(3, ft, at.y, k, at.partner).wait_send()
        p_swap.wait()

    for k in range(B_CHUNKS):
        for kind in range(3):
            b_copy(kind, ft, at.own_slab, k, at.mate).wait_send()


def spread_call(n, sources, lam, ft, pt):
    anywhere = pl.BlockSpec(memory_space=pl.ANY)
    rows = 2 * OO // n
    dma = pltpu.SemaphoreType.DMA
    return pl.pallas_call(
        functools.partial(spread_kernel, n),
        out_shape=(
            jax.ShapeDtypeStruct((OO, SLAB), BF),
            jax.ShapeDtypeStruct((OO, SLAB), BF),
            jax.ShapeDtypeStruct((4, SLAB, NAUX), BF),
            jax.ShapeDtypeStruct((SLAB, NAUX), BF),
        ),
        in_specs=[pl.BlockSpec(memory_space=pltpu.SMEM)] + [anywhere] * 3,
        out_specs=(anywhere,) * 4,
        scratch_shapes=[
            pltpu.VMEM((n, rows, SLAB // 2), BF),
            pltpu.VMEM((2, n, rows, SLAB // 2), BF),
            dma((n,)),
            dma((n,)),
            dma((2, n)),
            dma((2, n)),
            dma((4, B_CHUNKS)),
            dma((4, B_CHUNKS)),
            dma,
            dma,
            dma((2,)),
        ],
        compiler_params=pltpu.CompilerParams(collective_id=0, has_side_effects=True, vmem_limit_bytes=32 << 20),
        name="spread",
    )(sources, lam, ft, pt)


def widen_factor(raw, f):
    zero = jnp.zeros((PAD - V, NAUX), F32)

    def body(g):
        parts = [raw[s, rows_of(g, 2 * VS), :].astype(F32) for s in range(4)]
        out = []
        for h in range(2):
            out += [part[VS * h : VS * (h + 1)] for part in parts] + [zero]
        f[:, rows_of(g, 2 * PAD)] = jnp.concatenate(out, 0).astype(BF).T

    loop(V // 2, body)


FORM = 16


def form(left, f, w):
    def body(g):
        x = jnp.dot(left(), f[:, rows_of(g, FORM * PAD)], preferred_element_type=F32)
        for pair in range(VS // 2):
            two = x[2 * VS * pair : 2 * VS * (pair + 1)]
            for q in range(FORM // 2):
                lo = 2 * PAD * q
                even = jnp.concatenate([two[:VS, lo : lo + PAD], two[VS:, lo : lo + PAD]], 1)
                odd = jnp.concatenate([two[:VS, lo + PAD : lo + 2 * PAD], two[VS:, lo + PAD : lo + 2 * PAD]], 1)
                w[pair, pl.ds(pl.multiple_of(g * (FORM * VS) + 2 * VS * q, 2 * VS), 2 * VS), :] = jnp.concatenate(
                    [even, odd], 0
                ).astype(BF)

    loop(V // FORM, body)


def ladder(left, w, total, first):
    for pair in range(VS // 2):
        x = jnp.dot(left(), w[pair], preferred_element_type=F32)
        at = pl.ds(2 * PAD * pair, 2 * PAD)
        if first:
            total[:, at] = x
        else:
            total[:, at] += x


def work_kernel(
    lw, cyc, ptw, fall, g_in, out, raw, f, w, lall, gall, total, cycle, mine, theirs,
    l_send, l_recv, g_send, g_recv, o_send, o_recv, own_sem,
):
    at = Place()
    barrier = pltpu.get_barrier_semaphore()
    for device in (at.mate, at.cross, at.partner):
        pl.semaphore_signal(barrier, inc=1, device_id=device, device_id_type=MESH)
    pl.semaphore_wait(barrier, 3)

    def l_copy(kind, src, slab, device):
        return remote(src, lall.at[slab], l_send.at[kind], l_recv.at[kind], device)

    def g_copy(kind, src, slab, device):
        return remote(src, gall.at[slab], g_send.at[kind], g_recv.at[kind], device)

    l_copy(1, lw, at.own_slab, at.cross).start()
    l_copy(0, lw, at.own_slab, at.mate).start()
    l_own = pltpu.make_async_copy(lw, lall.at[at.own_slab], own_sem.at[0])
    f_own = pltpu.make_async_copy(fall, raw, own_sem.at[1])
    g_own = pltpu.make_async_copy(g_in, gall.at[at.own_slab], own_sem.at[2])
    f_own.start()
    l_own.start()

    @pl.when(at.home)
    def _():
        g_copy(1, g_in, at.own_slab, at.cross).start()
        g_copy(0, g_in, at.own_slab, at.mate).start()
        g_own.start()

    @pl.when(at.away)
    def _():
        g_copy(3, g_in, at.y, at.partner).start()

    def left(slab):
        return lambda: ptw[rows_of(slab, VS * VS), :]

    f_own.wait()
    widen_factor(raw, f)
    form(left(at.own_slab), f, w)
    l_own.wait()
    ladder(lambda: lall[at.own_slab], w, total, True)

    @pl.when(at.away)
    def _():
        g_copy(3, g_in, at.own_slab, at.partner).wait_recv()
        g_copy(1, gall.at[at.own_slab], at.own_slab, at.cross).start()
        g_copy(0, gall.at[at.own_slab], at.own_slab, at.mate).start()

    form(left(at.mate_slab), f, w)
    l_copy(0, lw, at.mate_slab, at.mate).wait_recv()
    ladder(lambda: lall[at.mate_slab], w, total, False)
    l_copy(1, lw, at.cross_slab, at.cross).wait_recv()
    l_copy(2, lall.at[at.cross_slab], at.cross_slab, at.mate).start()
    form(left(at.cross_slab), f, w)
    ladder(lambda: lall[at.cross_slab], w, total, False)
    form(left(at.diag_slab), f, w)
    l_copy(2, lw, at.diag_slab, at.mate).wait_recv()
    ladder(lambda: lall[at.diag_slab], w, total, False)

    g_copy(1, g_in, at.cross_slab, at.cross).wait_recv()
    g_copy(2, gall.at[at.cross_slab], at.cross_slab, at.mate).start()

    @pl.when(at.home)
    def _():
        g_own.wait()

    g_copy(0, g_in, at.mate_slab, at.mate).wait_recv()
    g_copy(2, g_in, at.diag_slab, at.mate).wait_recv()
    depth = VS * O

    def cycle_part(j):
        x = None
        for s in range(4):
            y = jnp.dot(cyc[:, depth * s : depth * (s + 1)], gall[s, :, rows_of(j, 4 * V)], preferred_element_type=F32)
            x = y if x is None else x + y
        cycle[:, rows_of(j, 4 * V)] = x

    loop(O // 4, cycle_part)

    def o_copy(m):
        cols = rows_of(m, 4 * V)
        return remote(mine.at[:, cols], theirs.at[:, cols], o_send.at[m], o_recv.at[m], at.partner)

    def finish(m):
        cols = []
        for r in range(4):
            rows = cycle[pl.ds(pl.multiple_of(m * (4 * O) + O * r, O), O), :]
            rows = jnp.concatenate([rows[:, V * j : V * (j + 1)] for j in range(O)], 0)
            lad = total[:, pl.ds(pl.multiple_of(m * (4 * PAD) + PAD * r, PAD), PAD)]
            cols.append(lad[:, :V] + rows)
        x = jnp.concatenate(cols, 1)

        @pl.when(at.home)
        def _():
            out[:, rows_of(m, 4 * V)] = x

        @pl.when(at.away)
        def _():
            mine[:, rows_of(m, 4 * V)] = x.astype(BF)
            o_copy(m).start()

    loop(VS // 4, finish)

    @pl.when(at.away)
    def _():
        def take(m):
            o_copy(m).wait_recv()
            out[:, rows_of(m, 4 * V)] = theirs[:, rows_of(m, 4 * V)].astype(F32)

        loop(VS // 4, take)
        loop(VS // 4, lambda m: o_copy(m).wait_send())
        g_copy(3, g_in, at.y, at.partner).wait_send()

    for kind in range(3):
        l_copy(kind, lw, at.own_slab, at.mate).wait_send()
        g_copy(kind, g_in, at.own_slab, at.mate).wait_send()


def work_call(lw, cyc, ptw, fall, g_in):
    anywhere = pl.BlockSpec(memory_space=pl.ANY)
    vmem = pl.BlockSpec(memory_space=pltpu.VMEM)
    dma = pltpu.SemaphoreType.DMA
    return pl.pallas_call(
        work_kernel,
        out_shape=jax.ShapeDtypeStruct((OO, SLAB), F32),
        in_specs=[anywhere, vmem, vmem, anywhere, anywhere],
        out_specs=vmem,
        scratch_shapes=[
            pltpu.VMEM((4, SLAB, NAUX), BF),
            pltpu.VMEM((NAUX, V * PAD), BF),
            pltpu.VMEM((VS // 2, SLAB, 2 * PAD), BF),
            pltpu.VMEM((4, OO, SLAB), BF),
            pltpu.VMEM((4, VS * O, O * V), BF),
            pltpu.VMEM((OO, VS * PAD), F32),
            pltpu.VMEM((VS * O, O * V), F32),
            pltpu.VMEM((OO, SLAB), BF),
            pltpu.VMEM((OO, SLAB), BF),
            dma((3,)),
            dma((3,)),
            dma((4,)),
            dma((4,)),
            dma((VS // 4,)),
            dma((VS // 4,)),
            dma((3,)),
        ],
        compiler_params=pltpu.CompilerParams(collective_id=1, has_side_effects=True, vmem_limit_bytes=63 << 20),
        name="work",
    )(lw, cyc, ptw, fall, g_in)


def local(n, lam, chol, cycle_int, sources):
    factor = chol[0].reshape(NAUX, VS, V)
    ft = jnp.transpose(factor, (2, 1, 0)).reshape(SLAB, NAUX)
    pt = jnp.transpose(factor.reshape(NAUX, VS, 4, VS), (2, 1, 3, 0)).reshape(SLAB, NAUX)
    lw, sw, fall, ptw = spread_call(n, sources, lam[0], ft, pt)
    lw = jnp.transpose(lw.reshape(O, O, VS, V), (1, 0, 3, 2)).reshape(OO, SLAB)
    cyc = jnp.transpose(sw.reshape(O, O, VS, V), (2, 0, 3, 1)).reshape(VS * O, V * O)
    out = work_call(lw, cyc, ptw, fall, cycle_int[0])
    out = jnp.transpose(out.reshape(O, O, SLAB), (1, 0, 2)).reshape(OO, SLAB)
    return out[None]


def solution(mesh):
    placed = (P("kpair", None, "vir"), P("kpair", None, "vir"), P("kpair", "vir", None), P())
    return jax.shard_map(
        functools.partial(local, mesh.shape["kpair"]),
        mesh=mesh,
        in_specs=placed,
        out_specs=P("kpair", None, "vir"),
        check_vma=False,
    )
```

time: 378 us -> 228 us (0.60)
  Pallas kernels: 0 us -> 168 us
  waiting for transfers between devices: 90.8 us -> 0 us
  matrix products: 89.2 us -> 0 us
  local copies, waits for them, and re-layouts: 133 us -> 59 us
  blocking collectives: 35.9 us -> 0 us
  between operations: 13.2 us -> 0.07 us
  starting transfers between devices: 9.53 us -> 0 us
    pallas_call x0 -> x2, Pallas kernels: none -> 168 us  [the longest x1 84.8 us: work_call(): pl.pallas_call(work_kernel, out_shape=jax.ShapeDtypeStruct((OO, SLAB), F3...]
    dot_general x7 -> x0, matrix products: 89.2 us -> none  [the longest x3 41 us: step(): lax.dot_general(ladder_full, block, (((1,), (1,)), ((), ())), preferred_e...]
    all_gather x3 -> x0, waiting for transfers between devices: 72.5 us -> none  [the longest x1 36.3 us: local(): lax.all_gather(factor_local, 'vir', axis=1, tiled=True).reshape(naux, V, V)]
    reshape x6, local copies, waits for them, and re-layouts: 96.5 us -> 45.2 us  [the longest x3 19.6 us: local(): lw = jnp.transpose(lw.reshape(O, O, VS, V), (1, 0, 3, 2)).reshape(OO, SLAB)]
    all_to_all x1 -> x0, blocking collectives: 35.9 us -> none  [local(): lax.all_to_all(chosen, 'kpair', split_axis=1, concat_axis=1, tiled=True)]
    all_to_all x1 -> x0, waiting for transfers between devices: 17.5 us -> none  [local(): lax.all_to_all(own.reshape(count, piece, width), 'kpair', split_axis=0, c...]
    while x1 -> x0, local copies, waits for them, and re-layouts: 10.3 us -> none  [local(): lax.fori_loop(0, slab // a_block, step, jnp.zeros((rows_all, slab, V), jn...]
    all_to_all x1 -> x0, starting transfers between devices: 9.45 us -> none  [local(): lax.all_to_all(own.reshape(count, piece, width), 'kpair', split_axis=0, c...]
  transfers between devices with their start and end apart: 4 -> 0, of which waited for: 3 -> 0; matrix products, arithmetic and copies ran while one was open for 14% -> 0% of each run, Pallas kernels for 0% -> 0%
where the time goes in v1:
time: 228 us; the launch traced here: 227 us
  Pallas kernels  168 us (74%)
  local copies, waits for them, and re-layouts  59 us (26%)
    pallas_call x1, Pallas kernels, work_call(): pl.pallas_call(work_kernel, out_shape=jax.ShapeDtypeStruct((OO, SLAB), F3...  84.8 us
    pallas_call x1, Pallas kernels, spread_call(): pl.pallas_call(functools.partial(spread_kernel, n), out_shape=(jax.ShapeD...  83.4 us
    reshape x3, local copies, waits for them, and re-layouts, local(): lw = jnp.transpose(lw.reshape(O, O, VS, V), (1, 0, 3, 2)).reshape(OO, SLAB)  19.6 us
    reshape x1, local copies, waits for them, and re-layouts, local(): jnp.transpose(sw.reshape(O, O, VS, V), (2, 0, 3, 1)).reshape(VS * O, V * O)  16.8 us
    reshape x2, local copies, waits for them, and re-layouts, local(): sw.reshape(O, O, VS, V)  8.75 us
    unnamed x8, local copies, waits for them, and re-layouts  8.63 us

profile of v1, /device:TPU:1, one launch (start us, length us, event | category | flops | bytes accessed | tf_op | source)
XLA Modules:
  0.0 227.2 jit_solution(1319341962574678835)
XLA Ops:
  0.0 0.8 copy.15.src
  0.8 2.8 %copy.11 = bf16[1,384,2304]{1,2,0:T(8,128)(2,1)S(1)} copy(bf16[1,384,2304]{2,1,0:T(8,128)(2,1)} %param.5) | data formatting | bytes 3538944 | tf_op args[1]
  3.5 0.6 copy.12
  4.1 0.0 copy-start.2
  4.2 0.2 copy.14
  4.3 1.1 copy-done.2
  5.4 83.4 %spread.1 = (bf16[256,2304]{1,0:T(8,128)(2,1)S(1)}, bf16[256,2304]{1,0:T(8,128)(2,1)S(1)}, bf16[4,2304,384]{2,1,0:T(8,128)(2,1)S(1)}, bf16[2304,384]{1,0:T(8,128)(2,1)S(1)}) custom-call(s32[32,2]{1,0:T(8,128)S(1)} %copy.15.src, bf16[256,2304]{1,0:T(8,128)(2,1)S(1)} %bitcast.22, bf16[2304,384]{1,0:T(8,128)(2,1)S(1)} %bitcast.20, bf16[2304,384]{1,0:T(8,128)(2,1)S(1)} %bitcast.21), custom_call_target="tpu_custom_call" | custom-call | tf_op jit(solution)/shard_map/spread/pallas_call | solution.py:219
  88.8 0.0 copy-start
  88.8 2.8 %copy-done = bf16[4,2304,384]{2,1,0:T(8,128)(2,1)} copy-done((bf16[4,2304,384]{2,1,0:T(8,128)(2,1)}, bf16[4,2304,384]{2,1,0:T(8,128)(2,1)S(1)}, u32[]{:S(2)}) %copy-start) | copy-done | bytes 7077912
  91.6 0.0 copy-start.1
  91.6 1.2 copy-done.1
  92.8 3.3 %reshape.23 = bf16[16,16,24,96]{3,2,1,0:T(8,128)(2,1)} reshape(bf16[256,2304]{1,0:T(8,128)(2,1)S(1)} %get-tuple-element.9) | data formatting | bytes 2359296 | tf_op jit(solution)/shard_map/reshape | solution.py:445
  96.1 2.4 %reshape.25 = bf16[16,16,24,96]{3,2,1,0:T(8,128)(2,1)S(1)} reshape(bf16[256,2304]{1,0:T(8,128)(2,1)S(1)} %get-tuple-element.10) | data formatting | bytes 2359296 | tf_op jit(solution)/shard_map/reshape | solution.py:446
  98.5 6.2 %copy.16 = bf16[16,16,24,96]{2,3,0,1:T(8,128)(2,1)} copy(bf16[16,16,24,96]{3,2,1,0:T(8,128)(2,1)} %reshape.23) | data formatting | bytes 2359296 | tf_op jit(solution)/shard_map/reshape | solution.py:445
  104.7 10.2 %reshape.24.lw = bf16[256,2304]{1,0:T(8,128)(2,1)} reshape(bf16[16,16,96,24]{3,2,1,0:T(8,128)(2,1)} %bitcast.24) | data formatting | bytes 2359296 | tf_op jit(solution)/shard_map/reshape | solution.py:445
  114.8 6.3 %copy.17 = bf16[16,16,24,96]{1,3,0,2:T(8,128)(2,1)} copy(bf16[16,16,24,96]{3,2,1,0:T(8,128)(2,1)S(1)} %reshape.25) | data formatting | bytes 2359296 | tf_op jit(solution)/shard_map/reshape | solution.py:446
  121.2 16.8 %reshape.26.cyc = bf16[384,1536]{1,0:T(8,128)(2,1)} reshape(bf16[24,16,96,16]{3,2,1,0:T(8,128)(2,1)} %bitcast.23) | data formatting | bytes 2359296 | tf_op jit(solution)/shard_map/reshape | solution.py:446
  138.0 84.8 %work.1 = f32[256,2304]{1,0:T(8,128)} custom-call(bf16[256,2304]{1,0:T(8,128)(2,1)} %reshape.24.lw, bf16[384,1536]{1,0:T(8,128)(2,1)} %reshape.26.cyc, bf16[2304,384]{1,0:T(8,128)(2,1)} %copy-done.1, bf16[4,2304,384]{2,1,0:T(8,128)(2,1)} %copy-done, bf16[384,1536]{1,0:T(8,128)(2,1)} %bitcast.28), custom_call_target="tpu_custom_call" | custom-call | tf_op jit(solution)/shard_map/work/pallas_call | solution.py:412
  222.8 4.4 %copy.18 = f32[16,16,2304]{2,1,0:T(8,128)} copy(f32[16,16,2304]{2,0,1:T(8,128)} %bitcast.27) | data formatting | bytes 4718592 | tf_op jit(solution)/shard_map/transpose | solution.py:448
Async XLA Ops:
  4.1 1.3 copy-start.2
  88.8 2.8 %copy-start = (bf16[4,2304,384]{2,1,0:T(8,128)(2,1)}, bf16[4,2304,384]{2,1,0:T(8,128)(2,1)S(1)}, u32[]{:S(2)}) copy-start(bf16[4,2304,384]{2,1,0:T(8,128)(2,1)S(1)} %get-tuple-element.12.fall) | copy-start | bytes 21233668
  91.6 1.2 copy-start.1

commit v2 on v1

--- a/solution.py
+++ b/solution.py
@@ -248,13 +248,53 @@
     zero = jnp.zeros((PAD - V, NAUX), F32)
 
     def body(g):
-        parts = [raw[s, rows_of(g, 2 * VS), :].astype(F32) for s in range(4)]
+        parts = [raw(s, rows_of(g, 2 * VS)).astype(F32) for s in range(4)]
         out = []
         for h in range(2):
             out += [part[VS * h : VS * (h + 1)] for part in parts] + [zero]
         f[:, rows_of(g, 2 * PAD)] = jnp.concatenate(out, 0).astype(BF).T
 
     loop(V // 2, body)
+
+
+def one_hot(size, outer, inner):
+    row = lax.broadcasted_iota(jnp.int32, (size, size), 0)
+    col = lax.broadcasted_iota(jnp.int32, (size, size), 1)
+    x = lax.shift_right_logical(col, inner.bit_length() - 1)
+    y = lax.bitwise_and(col, inner - 1)
+    return jnp.where(row == y * outer + x, 1.0, 0.0).astype(BF)
+
+
+def flip_pairs(lw, turned, flat):
+    wide = 4 * V
+    for g in range(SLAB // wide):
+        x = lw[:, wide * g : wide * (g + 1)].astype(F32).T
+        for h in range(2):
+            turned[h, wide * g : wide * (g + 1), :] = x[:, PAD * h : PAD * (h + 1)]
+    for g in range(V // O):
+        x = [
+            jnp.concatenate([turned[h, pl.ds(O * g + d, VS, stride=V), :] for d in range(O)], 0) for h in range(2)
+        ]
+        flat[:, wide * g : wide * (g + 1)] = jnp.concatenate(x, 1).astype(BF).T
+
+
+def cycle_left(sw, swap, cyc):
+    def body(g):
+        x = jnp.dot(swap, sw[:, rows_of(g, 4 * V)], preferred_element_type=F32)
+        for r in range(4):
+            for m in range(4):
+                part = [x[O * k : O * (k + 1), V * r : V * (r + 1)] for k in range(4 * m, 4 * m + 4)]
+                cyc[pl.ds(pl.multiple_of(g * (4 * O) + O * r, O), O), 4 * V * m : 4 * V * (m + 1)] = jnp.concatenate(
+                    part, 1
+                ).astype(BF)
+
+    loop(VS // 4, body)
+
+
+def cycle_right(gall, swap, cols, right):
+    parts = [jnp.dot(swap, gall[s, :, cols], preferred_element_type=F32) for s in range(4)]
+    for k in range(O):
+        right[V * k : V * (k + 1), :] = jnp.concatenate([part[VS * k : VS * (k + 1)] for part in parts], 0).astype(BF)
 
 
 FORM = 16
@@ -287,8 +327,8 @@
 
 
 def work_kernel(
-    lw, cyc, ptw, fall, g_in, out, raw, f, w, lall, gall, total, cycle, mine, theirs,
-    l_send, l_recv, g_send, g_recv, o_send, o_recv, own_sem,
+    lw, sw, ptw, fall, g_in, out, f, w, lall, gall, total, turned, cyc, right, cycle, tall, mine, theirs,
+    l_send, l_recv, g_send, g_recv, o_send, o_recv, own_sem, f_sem,
 ):
     at = Place()
     barrier = pltpu.get_barrier_semaphore()
@@ -296,19 +336,28 @@
         pl.semaphore_signal(barrier, inc=1, device_id=device, device_id_type=MESH)
     pl.semaphore_wait(barrier, 3)
 
-    def l_copy(kind, src, slab, device):
-        return remote(src, lall.at[slab], l_send.at[kind], l_recv.at[kind], device)
+    def l_copy(kind, slab, device):
+        return remote(lall.at[slab], lall.at[slab], l_send.at[kind], l_recv.at[kind], device)
 
     def g_copy(kind, src, slab, device):
         return remote(src, gall.at[slab], g_send.at[kind], g_recv.at[kind], device)
 
-    l_copy(1, lw, at.own_slab, at.cross).start()
-    l_copy(0, lw, at.own_slab, at.mate).start()
-    l_own = pltpu.make_async_copy(lw, lall.at[at.own_slab], own_sem.at[0])
-    f_own = pltpu.make_async_copy(fall, raw, own_sem.at[1])
-    g_own = pltpu.make_async_copy(g_in, gall.at[at.own_slab], own_sem.at[2])
-    f_own.start()
-    l_own.start()
+    g_own = pltpu.make_async_copy(g_in, gall.at[at.own_slab], own_sem)
+    wide = 2 * PAD
+    raw = []
+    for s in range(4):
+        raw.append(pltpu.make_async_copy(fall.at[s, :, pl.ds(0, wide)], w.at[2 * s], f_sem.at[s, 0]))
+        raw.append(
+            pltpu.make_async_copy(
+                fall.at[s, :, pl.ds(wide, NAUX - wide)], w.at[2 * s + 1, :, pl.ds(0, NAUX - wide)], f_sem.at[s, 1]
+            )
+        )
+    for copy in raw:
+        copy.start()
+
+    flip_pairs(lw, turned, lall.at[at.own_slab])
+    l_copy(1, at.own_slab, at.cross).start()
+    l_copy(0, at.own_slab, at.mate).start()
 
     @pl.when(at.home)
     def _():
@@ -323,10 +372,12 @@
     def left(slab):
         return lambda: ptw[rows_of(slab, VS * VS), :]
 
-    f_own.wait()
-    widen_factor(raw, f)
+    for copy in raw:
+        copy.wait()
+    widen_factor(
+        lambda s, rows: jnp.concatenate([w[2 * s, rows, :], w[2 * s + 1, rows, : NAUX - wide]], 1), f
+    )
     form(left(at.own_slab), f, w)
-    l_own.wait()
     ladder(lambda: lall[at.own_slab], w, total, True)
 
     @pl.when(at.away)
@@ -336,14 +387,15 @@
         g_copy(0, gall.at[at.own_slab], at.own_slab, at.mate).start()
 
     form(left(at.mate_slab), f, w)
-    l_copy(0, lw, at.mate_slab, at.mate).wait_recv()
+    l_copy(0, at.mate_slab, at.mate).wait_recv()
     ladder(lambda: lall[at.mate_slab], w, total, False)
-    l_copy(1, lw, at.cross_slab, at.cross).wait_recv()
-    l_copy(2, lall.at[at.cross_slab], at.cross_slab, at.mate).start()
+    l_copy(1, at.cross_slab, at.cross).wait_recv()
+    l_copy(2, at.cross_slab, at.mate).start()
     form(left(at.cross_slab), f, w)
     ladder(lambda: lall[at.cross_slab], w, total, False)
+    cycle_left(sw, one_hot(OO, O, O), cyc)
     form(left(at.diag_slab), f, w)
-    l_copy(2, lw, at.diag_slab, at.mate).wait_recv()
+    l_copy(2, at.diag_slab, at.mate).wait_recv()
     ladder(lambda: lall[at.diag_slab], w, total, False)
 
     g_copy(1, g_in, at.cross_slab, at.cross).wait_recv()
@@ -355,14 +407,12 @@
 
     g_copy(0, g_in, at.mate_slab, at.mate).wait_recv()
     g_copy(2, g_in, at.diag_slab, at.mate).wait_recv()
-    depth = VS * O
+    swap = one_hot(VS * O, VS, O)
 
     def cycle_part(j):
-        x = None
-        for s in range(4):
-            y = jnp.dot(cyc[:, depth * s : depth * (s + 1)], gall[s, :, rows_of(j, 4 * V)], preferred_element_type=F32)
-            x = y if x is None else x + y
-        cycle[:, rows_of(j, 4 * V)] = x
+        cols = rows_of(j, 4 * V)
+        cycle_right(gall, swap, cols, right)
+        cycle[:, cols] = jnp.dot(cyc[...], right[...], preferred_element_type=F32)
 
     loop(O // 4, cycle_part)
 
@@ -374,9 +424,10 @@
         cols = []
         for r in range(4):
             rows = cycle[pl.ds(pl.multiple_of(m * (4 * O) + O * r, O), O), :]
-            rows = jnp.concatenate([rows[:, V * j : V * (j + 1)] for j in range(O)], 0)
+            for j in range(O):
+                tall[r, pl.ds(j, O, stride=O), :V] = rows[:, V * j : V * (j + 1)]
             lad = total[:, pl.ds(pl.multiple_of(m * (4 * PAD) + PAD * r, PAD), PAD)]
-            cols.append(lad[:, :V] + rows)
+            cols.append(lad[:, :V] + tall[r, :, :V])
         x = jnp.concatenate(cols, 1)
 
         @pl.when(at.home)
@@ -401,27 +452,30 @@
         g_copy(3, g_in, at.y, at.partner).wait_send()
 
     for kind in range(3):
-        l_copy(kind, lw, at.own_slab, at.mate).wait_send()
+        l_copy(kind, at.own_slab, at.mate).wait_send()
         g_copy(kind, g_in, at.own_slab, at.mate).wait_send()
 
 
-def work_call(lw, cyc, ptw, fall, g_in):
+def work_call(lw, sw, ptw, fall, g_in):
     anywhere = pl.BlockSpec(memory_space=pl.ANY)
     vmem = pl.BlockSpec(memory_space=pltpu.VMEM)
     dma = pltpu.SemaphoreType.DMA
     return pl.pallas_call(
         work_kernel,
         out_shape=jax.ShapeDtypeStruct((OO, SLAB), F32),
-        in_specs=[anywhere, vmem, vmem, anywhere, anywhere],
+        in_specs=[vmem, vmem, vmem, anywhere, anywhere],
         out_specs=vmem,
         scratch_shapes=[
-            pltpu.VMEM((4, SLAB, NAUX), BF),
             pltpu.VMEM((NAUX, V * PAD), BF),
             pltpu.VMEM((VS // 2, SLAB, 2 * PAD), BF),
             pltpu.VMEM((4, OO, SLAB), BF),
             pltpu.VMEM((4, VS * O, O * V), BF),
             pltpu.VMEM((OO, VS * PAD), F32),
+            pltpu.VMEM((2, SLAB, PAD), F32),
+            pltpu.VMEM((VS * O, O * V), BF),
+            pltpu.VMEM((O * V, 4 * V), BF),
             pltpu.VMEM((VS * O, O * V), F32),
+            pltpu.VMEM((4, OO, PAD), F32),
             pltpu.VMEM((OO, SLAB), BF),
             pltpu.VMEM((OO, SLAB), BF),
             dma((3,)),
@@ -430,11 +484,12 @@
             dma((4,)),
             dma((VS // 4,)),
             dma((VS // 4,)),
-            dma((3,)),
+            dma,
+            dma((4, 2)),
         ],
         compiler_params=pltpu.CompilerParams(collective_id=1, has_side_effects=True, vmem_limit_bytes=63 << 20),
         name="work",
-    )(lw, cyc, ptw, fall, g_in)
+    )(lw, sw, ptw, fall, g_in)
 
 
 def local(n, lam, chol, cycle_int, sources):
@@ -442,10 +497,7 @@
     ft = jnp.transpose(factor, (2, 1, 0)).reshape(SLAB, NAUX)
     pt = jnp.transpose(factor.reshape(NAUX, VS, 4, VS), (2, 1, 3, 0)).reshape(SLAB, NAUX)
     lw, sw, fall, ptw = spread_call(n, sources, lam[0], ft, pt)
-    lw = jnp.transpose(lw.reshape(O, O, VS, V), (1, 0, 3, 2)).reshape(OO, SLAB)
-    cyc = jnp.transpose(sw.reshape(O, O, VS, V), (2, 0, 3, 1)).reshape(VS * O, V * O)
-    out = work_call(lw, cyc, ptw, fall, cycle_int[0])
-    out = jnp.transpose(out.reshape(O, O, SLAB), (1, 0, 2)).reshape(OO, SLAB)
+    out = work_call(lw, sw, ptw, fall, cycle_int[0])
     return out[None]
 
 

time: 228 us -> 189 us (0.83)
  local copies, waits for them, and re-layouts: 59 us -> 14.8 us
  Pallas kernels: 168 us -> 174 us
    reshape x6 -> x0, local copies, waits for them, and re-layouts: 45.2 us -> none  [the longest x3 19.6 us: local(): lw = jnp.transpose(lw.reshape(O, O, VS, V), (1, 0, 3, 2)).reshape(OO, SLAB)]
    pallas_call x1, Pallas kernels: 84.8 us -> 90.1 us  [work_call(): pl.pallas_call(work_kernel, out_shape=jax.ShapeDtypeStruct((OO, SLAB), F3...]
    unnamed x8 -> x13, local copies, waits for them, and re-layouts: 8.63 us -> 14 us
    transpose x1 -> x0, local copies, waits for them, and re-layouts: 4.44 us -> none  [local(): out = jnp.transpose(out.reshape(O, O, SLAB), (1, 0, 2)).reshape(OO, SLAB)]
where the time goes in v2:
time: 189 us; the launch traced here: 188 us
  Pallas kernels  174 us (92%)
  local copies, waits for them, and re-layouts  14.8 us (8%)
    pallas_call x1, Pallas kernels, work_call(): pl.pallas_call(work_kernel, out_shape=jax.ShapeDtypeStruct((OO, SLAB), F3...  90.1 us
    pallas_call x1, Pallas kernels, spread_call(): pl.pallas_call(functools.partial(spread_kernel, n), out_shape=(jax.ShapeD...  83.4 us
    unnamed x13, local copies, waits for them, and re-layouts  14 us

profile of v2, /device:TPU:1, one launch (start us, length us, event | category | flops | bytes accessed | tf_op | source)
XLA Modules:
  0.0 188.3 jit_solution(4212944824339562581)
XLA Ops:
  0.0 0.8 copy.12.src
  0.8 2.8 %copy.8 = bf16[1,384,2304]{1,2,0:T(8,128)(2,1)S(1)} copy(bf16[1,384,2304]{2,1,0:T(8,128)(2,1)} %param.5) | data formatting | bytes 3538944 | tf_op args[1]
  3.5 0.6 copy.9
  4.1 0.0 copy-start.4
  4.2 0.2 copy.11
  4.3 1.1 copy-done.4
  5.4 83.4 %spread.1 = (bf16[256,2304]{1,0:T(8,128)(2,1)S(1)}, bf16[256,2304]{1,0:T(8,128)(2,1)S(1)}, bf16[4,2304,384]{2,1,0:T(8,128)(2,1)S(1)}, bf16[2304,384]{1,0:T(8,128)(2,1)S(1)}) custom-call(s32[32,2]{1,0:T(8,128)S(1)} %copy.12.src, bf16[256,2304]{1,0:T(8,128)(2,1)S(1)} %bitcast.13, bf16[2304,384]{1,0:T(8,128)(2,1)S(1)} %bitcast.11, bf16[2304,384]{1,0:T(8,128)(2,1)S(1)} %bitcast.12), custom_call_target="tpu_custom_call" | custom-call | tf_op jit(solution)/shard_map/spread/pallas_call | solution.py:219
  88.8 0.0 copy-start
  88.8 2.9 %copy-done = bf16[4,2304,384]{2,1,0:T(8,128)(2,1)} copy-done((bf16[4,2304,384]{2,1,0:T(8,128)(2,1)}, bf16[4,2304,384]{2,1,0:T(8,128)(2,1)S(1)}, u32[]{:S(2)}) %copy-start) | copy-done | bytes 7077912
  91.7 0.0 copy-start.1
  91.7 1.2 copy-done.1
  92.9 0.0 copy-start.2
  92.9 1.0 copy-done.2
  93.9 0.0 copy-start.3
  93.9 1.0 copy-done.3
  94.9 90.1 %work.1 = f32[256,2304]{1,0:T(8,128)} custom-call(bf16[256,2304]{1,0:T(8,128)(2,1)} %copy-done.2, bf16[256,2304]{1,0:T(8,128)(2,1)} %copy-done.3, bf16[2304,384]{1,0:T(8,128)(2,1)} %copy-done.1, bf16[4,2304,384]{2,1,0:T(8,128)(2,1)} %copy-done, bf16[384,1536]{1,0:T(8,128)(2,1)} %bitcast.17), custom_call_target="tpu_custom_call" | custom-call | tf_op jit(solution)/shard_map/work/pallas_call | solution.py:463
  185.1 3.2 %copy.14 = f32[1,256,2304]{2,1,0:T(8,128)} copy(f32[1,256,2304]{2,1,0:T(8,128)} %bitcast.16) | data formatting | bytes 4718592
Async XLA Ops:
  4.1 1.3 copy-start.4
  88.8 2.9 %copy-start = (bf16[4,2304,384]{2,1,0:T(8,128)(2,1)}, bf16[4,2304,384]{2,1,0:T(8,128)(2,1)S(1)}, u32[]{:S(2)}) copy-start(bf16[4,2304,384]{2,1,0:T(8,128)(2,1)S(1)} %get-tuple-element.12.fall) | copy-start | bytes 21233668
  91.7 1.2 copy-start.1
  92.9 1.0 copy-start.2
  93.9 1.0 copy-start.3

commit v3 on v0

v3 whole, which is shorter than its diff:
```python
import functools

import jax
import jax.numpy as jnp
from jax import lax
from jax.experimental import pallas as pl
from jax.experimental.pallas import tpu as pltpu
from jax.sharding import PartitionSpec as P

O = 16
V = 96
VS = 24
NAUX = 384
OO = O * O
SLAB = VS * V
PAD = 128
BF = jnp.bfloat16
F32 = jnp.float32
MESH = pl.DeviceIdType.MESH
D_CHUNKS = 3
DC = V // D_CHUNKS
CROWS = DC * VS


class Place:
    def __init__(self):
        kp = lax.axis_index("kpair")
        y = lax.axis_index("vir")
        core = kp % 2
        half = y // 2
        guest = (core + half) % 2
        other = y + 1 - 2 * (y % 2)
        swap = kp + 1 - 2 * core
        self.kp, self.y, self.half, self.guest = kp, y, half, guest
        self.home = guest == 0
        self.away = guest == 1
        self.mate = (swap, y)
        self.cross = (kp, other)
        self.partner = (swap, 3 - y)
        self.own_slab = y + guest * (3 - 2 * y)
        self.mate_slab = y + (1 - guest) * (3 - 2 * y)
        self.cross_slab = other + guest * (3 - 2 * other)
        self.diag_slab = other + (1 - guest) * (3 - 2 * other)


def remote(src, dst, send, recv, device):
    return pltpu.make_async_remote_copy(
        src_ref=src, dst_ref=dst, send_sem=send, recv_sem=recv, device_id=device, device_id_type=MESH
    )


def loop(count, body):
    def step(i, carry):
        body(i)
        return carry

    lax.fori_loop(0, count, step, 0)


def rows_of(index, size):
    return pl.ds(pl.multiple_of(index * size, size), size)


def widen_factor(raw, f, k):
    zero = jnp.zeros((PAD - V, NAUX), F32)

    def body(g):
        parts = [
            raw[pl.ds(pl.multiple_of(g * (2 * VS) + CROWS * s, 2 * VS), 2 * VS), :].astype(F32) for s in range(4)
        ]
        out = []
        for h in range(2):
            out += [part[VS * h : VS * (h + 1)] for part in parts] + [zero]
        f[:, rows_of(g + k * (DC // 2), 2 * PAD)] = jnp.concatenate(out, 0).astype(BF).T

    loop(DC // 2, body)


FORM = 16


def form(left, f, k, w):
    def body(g):
        x = jnp.dot(left(), f[:, rows_of(g + k * (DC // FORM), FORM * PAD)], preferred_element_type=F32)
        for pair in range(VS // 2):
            two = x[2 * VS * pair : 2 * VS * (pair + 1)]
            for q in range(FORM // 2):
                lo = 2 * PAD * q
                even = jnp.concatenate([two[:VS, lo : lo + PAD], two[VS:, lo : lo + PAD]], 1)
                odd = jnp.concatenate([two[:VS, lo + PAD : lo + 2 * PAD], two[VS:, lo + PAD : lo + 2 * PAD]], 1)
                w[pair, pl.ds(pl.multiple_of(g * (FORM * VS) + 2 * VS * q, 2 * VS), 2 * VS), :] = jnp.concatenate(
                    [even, odd], 0
                ).astype(BF)

    loop(DC // FORM, body)


def ladder(left, w, total):
    for pair in range(VS // 2):
        total[:, 2 * PAD * pair : 2 * PAD * (pair + 1)] += jnp.dot(left(), w[pair], preferred_element_type=F32)


def one_hot(size, outer, inner):
    row = lax.broadcasted_iota(jnp.int32, (size, size), 0)
    col = lax.broadcasted_iota(jnp.int32, (size, size), 1)
    x = lax.shift_right_logical(col, inner.bit_length() - 1)
    y = lax.bitwise_and(col, inner - 1)
    return jnp.where(row == y * outer + x, 1.0, 0.0).astype(BF)


def first_factor(raw, plane, left):
    for h in range(NAUX // PAD):
        lanes = slice(PAD * h, PAD * (h + 1))
        plane[...] = raw[:SLAB, lanes].astype(F32)

        def body(s):
            for a in range(0, VS, 2):
                two = [plane[pl.ds(VS * VS * s + a + e, VS, stride=VS), :] for e in range(2)]
                left[pl.ds(pl.multiple_of(s * (VS * VS) + VS * a, 2 * VS), 2 * VS), lanes] = jnp.concatenate(
                    two, 0
                ).astype(BF)

        loop(4, body)


def flip_pairs(lw, plane, flat):
    wide = 4 * V
    for h in range(OO // PAD):
        rows = slice(PAD * h, PAD * (h + 1))
        for g in range(SLAB // wide):
            plane[wide * g : wide * (g + 1), :] = lw[rows, wide * g : wide * (g + 1)].astype(F32).T
        for g in range(V // O):
            x = jnp.concatenate([plane[pl.ds(O * g + d, VS, stride=V), :] for d in range(O)], 0)
            flat[rows, wide * g : wide * (g + 1)] = x.astype(BF).T


def cycle_left(sw, swap, cyc):
    def body(g):
        x = jnp.dot(swap, sw[:, rows_of(g, 4 * V)], preferred_element_type=F32)
        for r in range(4):
            for m in range(4):
                part = [x[O * k : O * (k + 1), V * r : V * (r + 1)] for k in range(4 * m, 4 * m + 4)]
                cyc[pl.ds(pl.multiple_of(g * (4 * O) + O * r, O), O), 4 * V * m : 4 * V * (m + 1)] = jnp.concatenate(
                    part, 1
                ).astype(BF)

    loop(VS // 4, body)


def cycle_right(part, swap, right):
    slabs = [jnp.dot(swap, part[s], preferred_element_type=F32) for s in range(4)]
    for k in range(O):
        right[V * k : V * (k + 1), :] = jnp.concatenate([x[VS * k : VS * (k + 1)] for x in slabs], 0).astype(BF)


G_CHUNKS = 4
GC = O * V // G_CHUNKS


def kernel(
    n, src, lam, ft, g_in, out, fall, gall, z, stage, lw, sw, raw, f, w, lall, total, plane, left, cyc, part, right,
    cycle, tall, mine, theirs, z_send, z_recv, w_send, w_recv, b_send, b_recv, l_send, l_recv, g_send, g_recv, o_send,
    o_recv, raw_sem, part_sem,
):
    at = Place()
    rows = 2 * OO // n
    lanes = SLAB // 2

    def piece(ref, q):
        return ref.at[rows_of(q // 2, rows), pl.ds(pl.multiple_of((q % 2) * lanes, 128), lanes)]

    barrier = pltpu.get_barrier_semaphore()

    def greet(o):
        pl.semaphore_signal(barrier, inc=1, device_id=((at.kp + o) % n, 3 - at.y), device_id_type=MESH)

    def greet_plane(o):
        pl.semaphore_signal(barrier, inc=1, device_id=((at.kp + o + 1) % n, at.y), device_id_type=MESH)

    pl.semaphore_signal(barrier, inc=1, device_id=at.cross, device_id_type=MESH)
    loop(n, greet)
    loop(n - 1, greet_plane)
    pl.semaphore_wait(barrier, 2 * n)

    def spread(o):
        q = (at.kp + o + 1) % n
        return remote(piece(lam, q), z.at[at.kp], z_send.at[q], z_recv.at[at.kp], (q, at.y))

    def spread_in(o):
        q = (at.kp + o + 1) % n
        return remote(piece(lam, at.kp), z.at[q], z_send.at[q], z_recv.at[q], (q, at.y))

    z_own = pltpu.make_async_copy(piece(lam, at.kp), z.at[at.kp], z_recv.at[at.kp])

    def place(kind, t):
        e = t % 2
        moved = (e + at.half) % 2
        device = (t + moved * (1 - 2 * e), at.y + moved * (3 - 2 * at.y))
        to = (lw, sw)[kind]
        return remote(stage.at[kind, t], piece(to, at.kp), w_send.at[kind, t], w_recv.at[kind, at.kp], device)

    def place_own(kind):
        return pltpu.make_async_copy(stage.at[kind, at.kp], piece((lw, sw)[kind], at.kp), w_recv.at[kind, at.kp])

    def place_in(kind, q):
        to = (lw, sw)[kind]
        return remote(stage.at[kind, q], piece(to, q), w_send.at[kind, q], w_recv.at[kind, q], at.partner)

    def send_picked(kind):
        def pick(t):
            stage[kind, t] = z[src[t, kind]]

        loop(n, pick)
        loop(n - 1, lambda o: place(kind, (at.kp + o + 1) % n).start())

        @pl.when(at.home)
        def _():
            place_own(kind).start()

        @pl.when(at.away)
        def _():
            place(kind, at.kp).start()

    def take_picked(kind):
        @pl.when(at.home)
        def _():
            loop(n - 1, lambda o: place_in(kind, (at.kp + o + 1) % n).wait_recv())
            place_own(kind).wait()

        @pl.when(at.away)
        def _():
            loop(n, lambda q: place_in(kind, q).wait_recv())

    def b_copy(kind, src_ref, slab, k, device):
        cut = pl.ds(CROWS * k, CROWS)
        return remote(src_ref.at[cut], fall.at[slab, cut], b_send.at[kind, k], b_recv.at[kind, k], device)

    def l_copy(kind, slab, device):
        return remote(lall.at[slab], lall.at[slab], l_send.at[kind], l_recv.at[kind], device)

    def g_copy(kind, src_ref, slab, j, device):
        cut = pl.ds(GC * j, GC)
        return remote(src_ref.at[:, cut], gall.at[slab, :, cut], g_send.at[kind, j], g_recv.at[kind, j], device)

    def fetch(mine, theirs, to, sem):
        @pl.when(at.home)
        def _():
            pltpu.make_async_copy(mine, to, sem).start()

        @pl.when(at.away)
        def _():
            pltpu.make_async_copy(theirs, to, sem).start()

    loop(n - 1, lambda o: spread(o).start())
    z_own.start()

    @pl.when(at.home)
    def _():
        for k in range(D_CHUNKS):
            b_copy(1, ft, at.own_slab, k, at.cross).start()
            b_copy(0, ft, at.own_slab, k, at.mate).start()

    @pl.when(at.away)
    def _():
        for k in range(D_CHUNKS):
            b_copy(3, ft, at.y, k, at.partner).start()
        for k in range(D_CHUNKS):
            b_copy(3, ft, at.own_slab, k, at.partner).wait_recv()
            b_copy(1, fall.at[at.own_slab], at.own_slab, k, at.cross).start()
            b_copy(0, fall.at[at.own_slab], at.own_slab, k, at.mate).start()
        for j in range(G_CHUNKS):
            g_copy(3, g_in, at.y, j, at.partner).start()

    def forward(k):
        b_copy(1, ft, at.cross_slab, k, at.cross).wait_recv()
        b_copy(2, fall.at[at.cross_slab], at.cross_slab, k, at.mate).start()

    def send_g(j):
        @pl.when(at.home)
        def _():
            g_copy(1, g_in, at.own_slab, j, at.cross).start()
            g_copy(0, g_in, at.own_slab, j, at.mate).start()

        @pl.when(at.away)
        def _():
            g_copy(3, g_in, at.own_slab, j, at.partner).wait_recv()
            g_copy(1, gall.at[at.own_slab], at.own_slab, j, at.cross).start()
            g_copy(0, gall.at[at.own_slab], at.own_slab, j, at.mate).start()

    def forward_g(j):
        g_copy(1, g_in, at.cross_slab, j, at.cross).wait_recv()
        g_copy(2, gall.at[at.cross_slab], at.cross_slab, j, at.mate).start()

    total[...] = jnp.zeros_like(total)

    fetch(ft, fall.at[at.own_slab], raw.at[pl.ds(0, SLAB)], raw_sem.at[0])
    pltpu.make_async_copy(ft, raw.at[pl.ds(0, SLAB)], raw_sem.at[0]).wait()
    first_factor(raw, plane, left)
    forward(0)
    loop(n - 1, lambda o: spread_in(o).wait_recv())
    z_own.wait()
    send_picked(0)

    def prepare(k):
        b_copy(0, ft, at.mate_slab, k, at.mate).wait_recv()
        b_copy(2, ft, at.diag_slab, k, at.mate).wait_recv()
        cut = pl.ds(CROWS * k, CROWS)
        slabs = (at.own_slab, at.mate_slab, at.cross_slab, at.diag_slab)
        copies = [
            pltpu.make_async_copy(fall.at[slab, cut], raw.at[rows_of(slab, CROWS)], raw_sem.at[i])
            for i, slab in enumerate(slabs)
        ]
        fetch(ft.at[cut], fall.at[at.own_slab, cut], raw.at[rows_of(at.own_slab, CROWS)], raw_sem.at[0])
        for copy in copies[1:]:
            copy.start()
        for copy in copies:
            copy.wait()
        widen_factor(raw, f, k)

    def pick_slab(far, e):
        near = (at.own_slab, at.mate_slab) if not far else (at.cross_slab, at.diag_slab)
        return near[0] + e * (near[1] - near[0])

    def form_pair(far, k, slot):
        def body(e):
            slab = pick_slab(far, e)
            form(lambda: left[rows_of(slab, VS * VS), :], f, k, w.at[slot + e])

        loop(2, body)

    def ladder_pairs(far, k, slot, count):
        def body(i):
            slab = pick_slab(far, i % 2)
            cut = rows_of(k + i // 2, CROWS)
            ladder(lambda: lall[slab, :, cut], w.at[slot + i], total)

        loop(2 * count, body)

    forward(1)
    prepare(0)
    form_pair(False, 0, 0)
    prepare(1)
    form_pair(False, 1, 2)
    forward(2)
    send_g(0)
    take_picked(0)
    flip_pairs(lw, plane, lall.at[at.own_slab])
    l_copy(1, at.own_slab, at.cross).start()
    l_copy(0, at.own_slab, at.mate).start()
    send_picked(1)
    l_copy(0, at.mate_slab, at.mate).wait_recv()
    ladder_pairs(False, 0, 0, 2)
    prepare(2)
    form_pair(False, 2, 0)
    ladder_pairs(False, 2, 0, 1)
    form_pair(True, 0, 0)
    for j in range(1, G_CHUNKS):
        send_g(j)
    form_pair(True, 1, 2)
    l_copy(1, at.cross_slab, at.cross).wait_recv()
    l_copy(2, at.cross_slab, at.mate).start()
    take_picked(1)
    cycle_left(sw, one_hot(OO, O, O), cyc)
    l_copy(2, at.diag_slab, at.mate).wait_recv()
    ladder_pairs(True, 0, 0, 2)
    forward_g(0)
    form_pair(True, 2, 0)
    ladder_pairs(True, 2, 0, 1)
    for j in range(1, G_CHUNKS):
        forward_g(j)

    swap = one_hot(VS * O, VS, O)
    for j in range(G_CHUNKS):
        g_copy(0, g_in, at.mate_slab, j, at.mate).wait_recv()
        g_copy(2, g_in, at.diag_slab, j, at.mate).wait_recv()

    def cycle_part(j):
        cols = rows_of(j, GC)
        slabs = (at.own_slab, at.mate_slab, at.cross_slab, at.diag_slab)
        copies = [
            pltpu.make_async_copy(gall.at[slab, :, cols], part.at[slab], part_sem.at[i])
            for i, slab in enumerate(slabs)
        ]
        fetch(g_in.at[:, cols], gall.at[at.own_slab, :, cols], part.at[at.own_slab], part_sem.at[0])
        for copy in copies[1:]:
            copy.start()
        for copy in copies:
            copy.wait()
        cycle_right(part, swap, right)
        cycle[:, cols] = jnp.dot(cyc[...], right[...], preferred_element_type=F32)

    loop(G_CHUNKS, cycle_part)

    def o_copy(m):
        cols = rows_of(m, 4 * V)
        return remote(mine.at[:, cols], theirs.at[:, cols], o_send.at[m], o_recv.at[m], at.partner)

    def finish(m):
        cols = []
        for r in range(4):
            some = cycle[pl.ds(pl.multiple_of(m * (4 * O) + O * r, O), O), :]
            for j in range(O):
                tall[r, pl.ds(j, O, stride=O), :V] = some[:, V * j : V * (j + 1)]
            lad = total[:, pl.ds(pl.multiple_of(m * (4 * PAD) + PAD * r, PAD), PAD)]
            cols.append(lad[:, :V] + tall[r, :, :V])
        x = jnp.concatenate(cols, 1)

        @pl.when(at.home)
        def _():
            out[:, rows_of(m, 4 * V)] = x

        @pl.when(at.away)
        def _():
            mine[:, rows_of(m, 4 * V)] = x.astype(BF)
            o_copy(m).start()

    loop(VS // 4, finish)

    @pl.when(at.away)
    def _():
        def take(m):
            o_copy(m).wait_recv()
            out[:, rows_of(m, 4 * V)] = theirs[:, rows_of(m, 4 * V)].astype(F32)

        loop(VS // 4, take)
        loop(VS // 4, lambda m: o_copy(m).wait_send())

    loop(n - 1, lambda o: spread(o).wait_send())
    for kind in range(2):
        loop(n - 1, lambda o: place(kind, (at.kp + o + 1) % n).wait_send())

    @pl.when(at.away)
    def _():
        for kind in range(2):
            place(kind, at.kp).wait_send()
        for k in range(D_CHUNKS):
            b_copy(3, ft, at.y, k, at.partner).wait_send()
        for j in range(G_CHUNKS):
            g_copy(3, g_in, at.y, j, at.partner).wait_send()

    for kind in range(3):
        l_copy(kind, at.own_slab, at.mate).wait_send()
        for k in range(D_CHUNKS):
            b_copy(kind, ft, at.own_slab, k, at.mate).wait_send()
        for j in range(G_CHUNKS):
            g_copy(kind, g_in, at.own_slab, j, at.mate).wait_send()


def call(n, sources, lam, ft, g_in):
    anywhere = pl.BlockSpec(memory_space=pl.ANY)
    dma = pltpu.SemaphoreType.DMA
    rows = 2 * OO // n
    out, _, _ = pl.pallas_call(
        functools.partial(kernel, n),
        out_shape=(
            jax.ShapeDtypeStruct((OO, SLAB), F32),
            jax.ShapeDtypeStruct((4, SLAB, NAUX), BF),
            jax.ShapeDtypeStruct((4, VS * O, O * V), BF),
        ),
        in_specs=[pl.BlockSpec(memory_space=pltpu.SMEM)] + [anywhere] * 3,
        out_specs=(pl.BlockSpec(memory_space=pltpu.VMEM), anywhere, anywhere),
        scratch_shapes=[
            pltpu.VMEM((n, rows, SLAB // 2), BF),
            pltpu.VMEM((2, n, rows, SLAB // 2), BF),
            pltpu.VMEM((OO, SLAB), BF),
            pltpu.VMEM((OO, SLAB), BF),
            pltpu.VMEM((4 * CROWS, NAUX), BF),
            pltpu.VMEM((NAUX, V * PAD), BF),
            pltpu.VMEM((4, VS // 2, CROWS, 2 * PAD), BF),
            pltpu.VMEM((4, OO, SLAB), BF),
            pltpu.VMEM((OO, VS * PAD), F32),
            pltpu.VMEM((SLAB, PAD), F32),
            pltpu.VMEM((SLAB, NAUX), BF),
            pltpu.VMEM((VS * O, O * V), BF),
            pltpu.VMEM((4, VS * O, GC), BF),
            pltpu.VMEM((O * V, GC), BF),
            pltpu.VMEM((VS * O, O * V), F32),
            pltpu.VMEM((4, OO, PAD), F32),
            pltpu.VMEM((OO, SLAB), BF),
            pltpu.VMEM((OO, SLAB), BF),
            dma((n,)),
            dma((n,)),
            dma((2, n)),
            dma((2, n)),
            dma((4, D_CHUNKS)),
            dma((4, D_CHUNKS)),
            dma((3,)),
            dma((3,)),
            dma((4, G_CHUNKS)),
            dma((4, G_CHUNKS)),
            dma((VS // 4,)),
            dma((VS // 4,)),
            dma((4,)),
            dma((4,)),
        ],
        compiler_params=pltpu.CompilerParams(collective_id=0, has_side_effects=True, vmem_limit_bytes=63 << 20),
        name="residual",
    )(sources, lam, ft, g_in)
    return out


def local(n, lam, chol, cycle_int, sources):
    ft = jnp.transpose(chol[0].reshape(NAUX, VS, V), (2, 1, 0)).reshape(SLAB, NAUX)
    return call(n, sources, lam[0], ft, cycle_int[0])[None]


def solution(mesh):
    placed = (P("kpair", None, "vir"), P("kpair", None, "vir"), P("kpair", "vir", None), P())
    return jax.shard_map(
        functools.partial(local, mesh.shape["kpair"]),
        mesh=mesh,
        in_specs=placed,
        out_specs=P("kpair", None, "vir"),
        check_vma=False,
    )
```

time: 378 us -> 158 us (0.42)
  Pallas kernels: 0 us -> 149 us
  local copies, waits for them, and re-layouts: 133 us -> 9.16 us
  waiting for transfers between devices: 90.8 us -> 0 us
  matrix products: 89.2 us -> 0 us
  blocking collectives: 35.9 us -> 0 us
  between operations: 13.2 us -> 0.02 us
  starting transfers between devices: 9.53 us -> 0 us
    pallas_call x0 -> x1, Pallas kernels: none -> 149 us  [call(): pl.pallas_call(functools.partial(kernel, n), out_shape=(jax.ShapeDtypeStr...]
    reshape x6 -> x0, local copies, waits for them, and re-layouts: 96.5 us -> none  [the longest x3 81.8 us: step(): block = block.astype(jnp.bfloat16).reshape(a_block, V * V, V)]
    dot_general x7 -> x0, matrix products: 89.2 us -> none  [the longest x3 41 us: step(): lax.dot_general(ladder_full, block, (((1,), (1,)), ((), ())), preferred_e...]
    all_gather x3 -> x0, waiting for transfers between devices: 72.5 us -> none  [the longest x1 36.3 us: local(): lax.all_gather(factor_local, 'vir', axis=1, tiled=True).reshape(naux, V, V)]
    all_to_all x1 -> x0, blocking collectives: 35.9 us -> none  [local(): lax.all_to_all(chosen, 'kpair', split_axis=1, concat_axis=1, tiled=True)]
    all_to_all x1 -> x0, waiting for transfers between devices: 17.5 us -> none  [local(): lax.all_to_all(own.reshape(count, piece, width), 'kpair', split_axis=0, c...]
    while x1 -> x0, local copies, waits for them, and re-layouts: 10.3 us -> none  [local(): lax.fori_loop(0, slab // a_block, step, jnp.zeros((rows_all, slab, V), jn...]
    all_to_all x1 -> x0, starting transfers between devices: 9.45 us -> none  [local(): lax.all_to_all(own.reshape(count, piece, width), 'kpair', split_axis=0, c...]
  transfers between devices with their start and end apart: 4 -> 0, of which waited for: 3 -> 0; matrix products, arithmetic and copies ran while one was open for 14% -> 0% of each run, Pallas kernels for 0% -> 0%
where the time goes in v3:
time: 158 us
  Pallas kernels  149 us (94%)
  local copies, waits for them, and re-layouts  9.16 us (6%)
    pallas_call x1, Pallas kernels, call(): pl.pallas_call(functools.partial(kernel, n), out_shape=(jax.ShapeDtypeStr...  149 us
    unnamed x3, local copies, waits for them, and re-layouts  7.33 us

profile of v3, /device:TPU:1, one launch (start us, length us, event | category | flops | bytes accessed | tf_op | source)
XLA Modules:
  0.0 157.9 jit_solution(12849009047212465862)
XLA Ops:
  0.0 1.4 copy.9.src
  1.4 2.8 %copy.7 = bf16[1,384,2304]{1,2,0:T(8,128)(2,1)S(1)} copy(bf16[1,384,2304]{2,1,0:T(8,128)(2,1)} %param.5) | data formatting | bytes 3538944 | tf_op args[1]
  4.1 1.8 %copy.8 = bf16[96,24,384]{2,1,0:T(8,128)(2,1)} copy(bf16[96,24,384]{2,0,1:T(8,128)(2,1)S(1)} %bitcast.7) | data formatting | bytes 3538944 | tf_op jit(solution)/shard_map/transpose | solution.py:503
  5.9 148.7 %residual.1 = (f32[256,2304]{1,0:T(8,128)}, bf16[4,2304,384]{2,1,0:T(8,128)(2,1)}, bf16[4,384,1536]{2,1,0:T(8,128)(2,1)}) custom-call(s32[32,2]{1,0:T(8,128)} %copy.9.src, bf16[256,2304]{1,0:T(8,128)(2,1)} %bitcast.10, bf16[2304,384]{1,0:T(8,128)(2,1)} %bitcast.8, bf16[384,1536]{1,0:T(8,128)(2,1)} %bitcast.11), custom_call_target="tpu_custom_call" | custom-call | tf_op jit(solution)/shard_map/residual/pallas_call | solution.py:453
  154.6 3.2 %copy.11 = f32[1,256,2304]{2,1,0:T(8,128)} copy(f32[1,256,2304]{2,1,0:T(8,128)} %bitcast.9) | data formatting | bytes 4718592

commit v4 on v3

v4 whole, which is shorter than its diff:
```python
import functools

import jax
import jax.numpy as jnp
from jax import lax
from jax.experimental import pallas as pl
from jax.experimental.pallas import tpu as pltpu
from jax.sharding import PartitionSpec as P

O = 16
V = 96
VS = 24
NAUX = 384
OO = O * O
SLAB = VS * V
PAD = 128
BF = jnp.bfloat16
F32 = jnp.float32
MESH = pl.DeviceIdType.MESH
D_CHUNKS = 3
DC = V // D_CHUNKS
CROWS = DC * VS


class Place:
    def __init__(self):
        kp = lax.axis_index("kpair")
        y = lax.axis_index("vir")
        core = kp % 2
        half = y // 2
        guest = (core + half) % 2
        other = y + 1 - 2 * (y % 2)
        swap = kp + 1 - 2 * core
        self.kp, self.y, self.half, self.guest = kp, y, half, guest
        self.home = guest == 0
        self.away = guest == 1
        self.mate = (swap, y)
        self.cross = (kp, other)
        self.partner = (swap, 3 - y)
        self.own_slab = y + guest * (3 - 2 * y)
        self.mate_slab = y + (1 - guest) * (3 - 2 * y)
        self.cross_slab = other + guest * (3 - 2 * other)
        self.diag_slab = other + (1 - guest) * (3 - 2 * other)


def remote(src, dst, send, recv, device):
    return pltpu.make_async_remote_copy(
        src_ref=src, dst_ref=dst, send_sem=send, recv_sem=recv, device_id=device, device_id_type=MESH
    )


def loop(count, body):
    def step(i, carry):
        body(i)
        return carry

    lax.fori_loop(0, count, step, 0)


def rows_of(index, size):
    return pl.ds(pl.multiple_of(index * size, size), size)


def merge_factor(raw, f, k):
    def body(g):
        parts = [
            raw[pl.ds(pl.multiple_of(g * (4 * VS) + CROWS * s, 2 * VS), 4 * VS), :].astype(F32) for s in range(4)
        ]
        out = [part[VS * h : VS * (h + 1)] for h in range(4) for part in parts]
        f[:, rows_of(g + k * (DC // 4), 4 * V)] = jnp.concatenate(out, 0).astype(BF).T

    loop(DC // 4, body)


PAIRS = 4


def form(left, f, k, w):
    lane = lax.broadcasted_iota(jnp.int32, (2 * VS, PAD), 1)

    def body(m):
        x = jnp.dot(left(m), f[:, rows_of(k, DC * V)], preferred_element_type=F32)
        for pair in range(PAIRS):
            two = x[2 * VS * pair : 2 * VS * (pair + 1)]
            for q in range(DC // 4):
                v = [two[:, 4 * V * q + PAD * e : 4 * V * q + PAD * (e + 1)] for e in range(3)]
                d = [
                    v[0],
                    jnp.where(lane < 32, pltpu.roll(v[0], 32, 1), pltpu.roll(v[1], 32, 1)),
                    jnp.where(lane < 64, pltpu.roll(v[1], 64, 1), pltpu.roll(v[2], 64, 1)),
                    pltpu.roll(v[2], 96, 1),
                ]
                d = [jnp.concatenate([y[:VS], y[VS:]], 1) for y in d]
                w[PAIRS * m + pair, 4 * VS * q : 4 * VS * (q + 1), :] = jnp.concatenate(d, 0).astype(BF)

    loop(VS // 2 // PAIRS, body)


def ladder(left, w, total):
    for pair in range(VS // 2):
        total[:, 2 * PAD * pair : 2 * PAD * (pair + 1)] += jnp.dot(left(), w[pair], preferred_element_type=F32)


def one_hot(size, outer, inner):
    row = lax.broadcasted_iota(jnp.int32, (size, size), 0)
    col = lax.broadcasted_iota(jnp.int32, (size, size), 1)
    x = lax.shift_right_logical(col, inner.bit_length() - 1)
    y = lax.bitwise_and(col, inner - 1)
    return jnp.where(row == y * outer + x, 1.0, 0.0).astype(BF)


def first_factor(raw, plane, left):
    for h in range(NAUX // PAD):
        lanes = slice(PAD * h, PAD * (h + 1))
        plane[...] = raw[:SLAB, lanes].astype(F32)

        def body(s):
            for a in range(0, VS, 2):
                two = [plane[pl.ds(VS * VS * s + a + e, VS, stride=VS), :] for e in range(2)]
                left[pl.ds(pl.multiple_of(s * (VS * VS) + VS * a, 2 * VS), 2 * VS), lanes] = jnp.concatenate(
                    two, 0
                ).astype(BF)

        loop(4, body)


def flip_factor(raw, plane, ft):
    wide = 4 * V
    for h in range(NAUX // PAD):
        for g in range(SLAB // wide):
            lo = NAUX * g + PAD * h
            plane[wide * g : wide * (g + 1), :] = raw[lo : lo + PAD, :].astype(F32).T

        def body(d):
            two = [plane[pl.ds(2 * d + e, VS, stride=V), :] for e in range(2)]
            ft[rows_of(d, 2 * VS), PAD * h : PAD * (h + 1)] = jnp.concatenate(two, 0).astype(BF)

        loop(V // 2, body)


def flip_pairs(lw, swap, plane, flat):
    wide = 4 * V
    for h in range(OO // PAD):
        rows = slice(PAD * h, PAD * (h + 1))
        for g in range(SLAB // wide):
            x = jnp.dot(swap[rows], lw[:, wide * g : wide * (g + 1)], preferred_element_type=F32)
            plane[wide * g : wide * (g + 1), :] = x.T
        for g in range(V // O):
            x = jnp.concatenate([plane[pl.ds(O * g + d, VS, stride=V), :] for d in range(O)], 0)
            flat[rows, wide * g : wide * (g + 1)] = x.astype(BF).T


def cycle_left(sw, swap, cyc):
    def body(g):
        x = jnp.dot(swap, sw[:, rows_of(g, 4 * V)], preferred_element_type=F32)
        for r in range(4):
            for m in range(4):
                part = [x[O * k : O * (k + 1), V * r : V * (r + 1)] for k in range(4 * m, 4 * m + 4)]
                cyc[pl.ds(pl.multiple_of(g * (4 * O) + O * r, O), O), 4 * V * m : 4 * V * (m + 1)] = jnp.concatenate(
                    part, 1
                ).astype(BF)

    loop(VS // 4, body)


def cycle_right(part, swap, right):
    slabs = [jnp.dot(swap, part(s), preferred_element_type=F32) for s in range(4)]
    for k in range(O):
        right[V * k : V * (k + 1), :] = jnp.concatenate([x[VS * k : VS * (k + 1)] for x in slabs], 0).astype(BF)


G_CHUNKS = 4
SLOTS = 5
GC = O * V // G_CHUNKS


def kernel(
    n, src, lam, chol, g_in, out, fall, gall, z, stage, lw, sw, raw, ft, f, w, lall, total, plane, left, cyc, more,
    cycle, theirs, z_send, z_recv, w_send, w_recv, b_send, b_recv, l_send, l_recv, g_send, g_recv, o_send, o_recv,
    raw_sem, part_sem,
):
    at = Place()
    rows = 2 * OO // n
    lanes = SLAB // 2

    def piece(ref, q):
        return ref.at[rows_of(q // 2, rows), pl.ds(pl.multiple_of((q % 2) * lanes, 128), lanes)]

    chol_in = [
        pltpu.make_async_copy(chol.at[:, pl.ds(NAUX * g, NAUX)], raw.at[pl.ds(NAUX * g, NAUX)], raw_sem.at[g])
        for g in range(SLAB // NAUX)
    ]
    for copy in chol_in:
        copy.start()
    barrier = pltpu.get_barrier_semaphore()

    def greet(o):
        pl.semaphore_signal(barrier, inc=1, device_id=((at.kp + o) % n, 3 - at.y), device_id_type=MESH)

    def greet_plane(o):
        pl.semaphore_signal(barrier, inc=1, device_id=((at.kp + o + 1) % n, at.y), device_id_type=MESH)

    pl.semaphore_signal(barrier, inc=1, device_id=at.cross, device_id_type=MESH)
    loop(n, greet)
    loop(n - 1, greet_plane)
    for copy in chol_in:
        copy.wait()
    flip_factor(raw, plane, ft)

    @pl.when(at.home)
    def _():
        first_factor(ft, plane, left)

    total[...] = jnp.zeros_like(total)
    pl.semaphore_wait(barrier, 2 * n)

    def spread(o):
        q = (at.kp + o + 1) % n
        return remote(piece(lam, q), z.at[at.kp], z_send.at[q], z_recv.at[at.kp], (q, at.y))

    def spread_in(o):
        q = (at.kp + o + 1) % n
        return remote(piece(lam, at.kp), z.at[q], z_send.at[q], z_recv.at[q], (q, at.y))

    z_own = pltpu.make_async_copy(piece(lam, at.kp), z.at[at.kp], z_recv.at[at.kp])

    def place(kind, t):
        e = t % 2
        moved = (e + at.half) % 2
        device = (t + moved * (1 - 2 * e), at.y + moved * (3 - 2 * at.y))
        to = (lw, sw)[kind]
        return remote(stage.at[t], piece(to, at.kp), w_send.at[kind, t], w_recv.at[kind, at.kp], device)

    def place_own(kind):
        return pltpu.make_async_copy(stage.at[at.kp], piece((lw, sw)[kind], at.kp), w_recv.at[kind, at.kp])

    def place_in(kind, q):
        to = (lw, sw)[kind]
        return remote(stage.at[q], piece(to, q), w_send.at[kind, q], w_recv.at[kind, q], at.partner)

    def send_picked(kind):
        def pick(t):
            stage[t] = z[src[kind, t]]

        loop(n, pick)
        loop(n - 1, lambda o: place(kind, (at.kp + o + 1) % n).start())

        @pl.when(at.home)
        def _():
            place_own(kind).start()

        @pl.when(at.away)
        def _():
            place(kind, at.kp).start()

    def sent_picked(kind):
        loop(n - 1, lambda o: place(kind, (at.kp + o + 1) % n).wait_send())

        @pl.when(at.away)
        def _():
            place(kind, at.kp).wait_send()

    def take_picked(kind):
        @pl.when(at.home)
        def _():
            loop(n - 1, lambda o: place_in(kind, (at.kp + o + 1) % n).wait_recv())
            place_own(kind).wait()

        @pl.when(at.away)
        def _():
            loop(n, lambda q: place_in(kind, q).wait_recv())

    def b_copy(kind, src_ref, slab, k, device):
        cut = pl.ds(CROWS * k, CROWS)
        return remote(src_ref.at[cut], fall.at[slab, cut], b_send.at[kind, k], b_recv.at[kind, k], device)

    def l_copy(kind, slab, device):
        return remote(lall.at[slab], lall.at[slab], l_send.at[kind], l_recv.at[kind], device)

    def g_copy(kind, src_ref, slab, j, device):
        cut = pl.ds(GC * j, GC)
        return remote(src_ref.at[:, cut], gall.at[slab, :, cut], g_send.at[kind, j], g_recv.at[kind, j], device)

    def fetch(mine, theirs, to, sem):
        @pl.when(at.home)
        def _():
            pltpu.make_async_copy(mine, to, sem).start()

        @pl.when(at.away)
        def _():
            pltpu.make_async_copy(theirs, to, sem).start()

    def issue(k):
        @pl.when(at.home)
        def _():
            b_copy(1, ft, at.own_slab, k, at.cross).start()
            b_copy(0, ft, at.own_slab, k, at.mate).start()

    def relay(k):
        @pl.when(at.away)
        def _():
            b_copy(3, ft, at.own_slab, k, at.partner).wait_recv()
            b_copy(1, fall.at[at.own_slab], at.own_slab, k, at.cross).start()
            b_copy(0, fall.at[at.own_slab], at.own_slab, k, at.mate).start()

    def swap_factor(k):
        @pl.when(at.away)
        def _():
            b_copy(3, ft, at.y, k, at.partner).start()

    def wait_diag(k):
        b_copy(2, ft, at.diag_slab, k, at.mate).wait_recv()

    def forward(k):
        b_copy(1, ft, at.cross_slab, k, at.cross).wait_recv()
        b_copy(2, fall.at[at.cross_slab], at.cross_slab, k, at.mate).start()

    def send_g(j):
        @pl.when(at.home)
        def _():
            g_copy(1, g_in, at.own_slab, j, at.cross).start()
            g_copy(0, g_in, at.own_slab, j, at.mate).start()

        @pl.when(at.away)
        def _():
            g_copy(3, g_in, at.own_slab, j, at.partner).wait_recv()
            g_copy(1, gall.at[at.own_slab], at.own_slab, j, at.cross).start()
            g_copy(0, gall.at[at.own_slab], at.own_slab, j, at.mate).start()

    def forward_g(j):
        g_copy(1, g_in, at.cross_slab, j, at.cross).wait_recv()
        g_copy(2, gall.at[at.cross_slab], at.cross_slab, j, at.mate).start()

    for k in range(D_CHUNKS):
        issue(k)
        swap_factor(k)
    loop(n - 1, lambda o: spread(o).start())
    z_own.start()
    relay(0)
    forward(0)
    wait_diag(0)
    relay(1)
    loop(n - 1, lambda o: spread_in(o).wait_recv())
    z_own.wait()
    send_picked(0)
    relay(2)

    @pl.when(at.away)
    def _():
        for j in range(G_CHUNKS):
            g_copy(3, g_in, at.y, j, at.partner).start()
        copy = pltpu.make_async_copy(fall.at[at.own_slab], raw.at[pl.ds(0, SLAB)], raw_sem.at[0])
        copy.start()
        copy.wait()
        first_factor(raw, plane, left)

    def prepare(k):
        b_copy(0, ft, at.mate_slab, k, at.mate).wait_recv()
        cut = pl.ds(CROWS * k, CROWS)
        slabs = (at.own_slab, at.mate_slab, at.cross_slab, at.diag_slab)
        copies = [
            pltpu.make_async_copy(fall.at[slab, cut], raw.at[rows_of(slab, CROWS)], raw_sem.at[i])
            for i, slab in enumerate(slabs)
        ]
        fetch(ft.at[cut], fall.at[at.own_slab, cut], raw.at[rows_of(at.own_slab, CROWS)], raw_sem.at[0])
        for copy in copies[1:]:
            copy.start()
        for copy in copies:
            copy.wait()
        merge_factor(raw, f, k)

    def pick_slab(far, e):
        two = (at.cross_slab, at.diag_slab) if far else (at.own_slab, at.mate_slab)
        return two[0] + e * (two[1] - two[0])

    def form_blocks(far, first, count):
        def body(i):
            b = first + i
            slab = pick_slab(far, b % 2)

            def rows(m):
                size = 2 * VS * PAIRS
                return left[rows_of(slab * (VS // 2 // PAIRS) + m, size), :]

            form(rows, f, b // 2, w.at[b % SLOTS])

        loop(count, body)

    def ladder_blocks(far, first, count):
        def body(i):
            b = first + i
            slab = pick_slab(far, b % 2)
            cut = rows_of(b // 2, CROWS)
            ladder(lambda: lall[slab, :, cut], w.at[b % SLOTS], total)

        loop(count, body)

    last = 2 * D_CHUNKS - SLOTS
    prepare(0)
    form_blocks(False, 0, 2)
    forward(1)
    wait_diag(1)
    prepare(1)
    form_blocks(False, 2, 2)
    forward(2)
    send_g(0)
    send_g(1)
    wait_diag(2)
    prepare(2)
    form_blocks(False, 4, SLOTS - 4)
    take_picked(0)
    swap_rows = one_hot(OO, O, O)
    flip_pairs(lw, swap_rows, plane, lall.at[at.own_slab])
    l_copy(1, at.own_slab, at.cross).start()
    l_copy(0, at.own_slab, at.mate).start()
    sent_picked(0)

    send_picked(1)
    l_copy(0, at.mate_slab, at.mate).wait_recv()
    ladder_blocks(False, 0, SLOTS)
    form_blocks(False, SLOTS, last)
    ladder_blocks(False, SLOTS, last)
    form_blocks(True, 0, SLOTS - 2)
    send_g(2)
    send_g(3)
    form_blocks(True, SLOTS - 2, 2)
    take_picked(1)
    cycle_left(sw, one_hot(OO, O, O), cyc)
    l_copy(1, at.cross_slab, at.cross).wait_recv()
    l_copy(2, at.cross_slab, at.mate).start()
    forward_g(0)
    forward_g(1)
    l_copy(2, at.diag_slab, at.mate).wait_recv()
    ladder_blocks(True, 0, SLOTS)

    half = O * V

    def part_of(j):
        return raw.at[pl.ds(half, half)] if j % 2 == 0 else more

    def part_copy(j, i):
        slab = (at.own_slab, at.mate_slab, at.cross_slab, at.diag_slab)[i]
        cols = pl.ds(GC * j, GC)
        to = part_of(j).at[rows_of(slab, VS * O)]
        return pltpu.make_async_copy(gall.at[slab, :, cols], to, part_sem.at[j % 2, i])

    def take_g(j):
        g_copy(0, g_in, at.mate_slab, j, at.mate).wait_recv()
        g_copy(2, g_in, at.diag_slab, j, at.mate).wait_recv()
        cols = pl.ds(GC * j, GC)
        to = part_of(j).at[rows_of(at.own_slab, VS * O)]
        fetch(g_in.at[:, cols], gall.at[at.own_slab, :, cols], to, part_sem.at[j % 2, 0])
        for i in range(1, 4):
            part_copy(j, i).start()

    def o_copy(j):
        cut = pl.ds(4 * O * j, 4 * O)
        return remote(lw.at[cut], theirs.at[cut], o_send.at[j], o_recv.at[j], at.partner)

    def finish(j):
        for i in range(4):
            part_copy(j, i).wait()
        swap = one_hot(VS * O, VS, O)
        cycle_right(lambda s: part_of(j)[VS * O * s : VS * O * (s + 1), :], swap, raw)
        cycle[...] = jnp.dot(cyc[...], raw[:half, :], preferred_element_type=F32)
        def body(m):
            cyc_rows = cycle[rows_of(m, 4 * O), :]
            for r in range(4):
                rows = slice(O * (4 * j + r), O * (4 * j + r + 1))
                lad = total[rows, rows_of(m, 4 * PAD)]
                x = [
                    lad[:, PAD * e : PAD * e + V] + cyc_rows[O * e : O * (e + 1), V * r : V * (r + 1)] for e in range(4)
                ]
                x = jnp.concatenate(x, 1)
                out[rows, rows_of(m, 4 * V)] = x
                lw[rows, rows_of(m, 4 * V)] = x.astype(BF)

        loop(VS // 4, body)

        @pl.when(at.away)
        def _():
            o_copy(j).start()

    take_g(0)
    take_g(1)
    form_blocks(True, SLOTS, last)
    ladder_blocks(True, SLOTS, last)
    finish(0)
    forward_g(2)
    take_g(2)
    finish(1)
    forward_g(3)
    take_g(3)
    finish(2)
    finish(3)

    @pl.when(at.away)
    def _():
        for j in range(G_CHUNKS):
            cut = slice(4 * O * j, 4 * O * (j + 1))
            o_copy(j).wait_recv()
            out[cut, :] = theirs[cut, :].astype(F32)
        for j in range(G_CHUNKS):
            o_copy(j).wait_send()

    loop(n - 1, lambda o: spread(o).wait_send())
    sent_picked(1)

    @pl.when(at.away)
    def _():
        for k in range(D_CHUNKS):
            b_copy(3, ft, at.y, k, at.partner).wait_send()
        for j in range(G_CHUNKS):
            g_copy(3, g_in, at.y, j, at.partner).wait_send()

    for kind in range(3):
        l_copy(kind, at.own_slab, at.mate).wait_send()
        for k in range(D_CHUNKS):
            b_copy(kind, ft, at.own_slab, k, at.mate).wait_send()
        for j in range(G_CHUNKS):
            g_copy(kind, g_in, at.own_slab, j, at.mate).wait_send()


def call(n, sources, lam, chol, g_in):
    anywhere = pl.BlockSpec(memory_space=pl.ANY)
    dma = pltpu.SemaphoreType.DMA
    rows = 2 * OO // n
    out, _, _ = pl.pallas_call(
        functools.partial(kernel, n),
        out_shape=(
            jax.ShapeDtypeStruct((OO, SLAB), F32),
            jax.ShapeDtypeStruct((4, SLAB, NAUX), BF),
            jax.ShapeDtypeStruct((4, VS * O, O * V), BF),
        ),
        in_specs=[pl.BlockSpec(memory_space=pltpu.SMEM)] + [anywhere] * 3,
        out_specs=(pl.BlockSpec(memory_space=pltpu.VMEM), anywhere, anywhere),
        scratch_shapes=[
            pltpu.VMEM((n, rows, SLAB // 2), BF),
            pltpu.VMEM((n, rows, SLAB // 2), BF),
            pltpu.VMEM((OO, SLAB), BF),
            pltpu.VMEM((OO, SLAB), BF),
            pltpu.VMEM((4 * CROWS, NAUX), BF),
            pltpu.VMEM((SLAB, NAUX), BF),
            pltpu.VMEM((NAUX, V * V), BF),
            pltpu.VMEM((SLOTS, VS // 2, CROWS, 2 * PAD), BF),
            pltpu.VMEM((4, OO, SLAB), BF),
            pltpu.VMEM((OO, VS * PAD), F32),
            pltpu.VMEM((SLAB, PAD), F32),
            pltpu.VMEM((SLAB, NAUX), BF),
            pltpu.VMEM((VS * O, O * V), BF),
            pltpu.VMEM((O * V, GC), BF),
            pltpu.VMEM((VS * O, GC), F32),
            pltpu.VMEM((OO, SLAB), BF),
            dma((n,)),
            dma((n,)),
            dma((2, n)),
            dma((2, n)),
            dma((4, D_CHUNKS)),
            dma((4, D_CHUNKS)),
            dma((3,)),
            dma((3,)),
            dma((4, G_CHUNKS)),
            dma((4, G_CHUNKS)),
            dma((G_CHUNKS,)),
            dma((G_CHUNKS,)),
            dma((SLAB // NAUX,)),
            dma((2, 4)),
        ],
        compiler_params=pltpu.CompilerParams(collective_id=0, has_side_effects=True, vmem_limit_bytes=63 << 20),
        name="residual",
    )(jnp.transpose(sources), lam, chol, g_in)
    return out


def local(n, lam, chol, cycle_int, sources):
    out = call(n, sources, lam[0], chol[0], cycle_int[0])
    return jnp.transpose(out.reshape(O, O, SLAB), (1, 0, 2)).reshape(1, OO, SLAB)


def solution(mesh):
    placed = (P("kpair", None, "vir"), P("kpair", None, "vir"), P("kpair", "vir", None), P())
    return jax.shard_map(
        functools.partial(local, mesh.shape["kpair"]),
        mesh=mesh,
        in_specs=placed,
        out_specs=P("kpair", None, "vir"),
        check_vma=False,
    )
```

time: 158 us -> 143 us (0.905)
  Pallas kernels: 149 us -> 138 us
  local copies, waits for them, and re-layouts: 9.16 us -> 4.44 us
    pallas_call x1, Pallas kernels: 149 us -> 138 us  [call(): pl.pallas_call(functools.partial(kernel, n), out_shape=(jax.ShapeDtypeStr...]
    unnamed x3 -> x0, local copies, waits for them, and re-layouts: 7.33 us -> none
    transpose x1, local copies, waits for them, and re-layouts: 1.83 us -> 4.44 us  [local(): jnp.transpose(out.reshape(O, O, SLAB), (1, 0, 2)).reshape(1, OO, SLAB)]
where the time goes in v4:
time: 143 us
  Pallas kernels  138 us (97%)
  local copies, waits for them, and re-layouts  4.44 us (3%)
    pallas_call x1, Pallas kernels, call(): pl.pallas_call(functools.partial(kernel, n), out_shape=(jax.ShapeDtypeStr...  138 us
    transpose x1, local copies, waits for them, and re-layouts, local(): jnp.transpose(out.reshape(O, O, SLAB), (1, 0, 2)).reshape(1, OO, SLAB)  4.44 us

profile of v4, /device:TPU:1, one launch (start us, length us, event | category | flops | bytes accessed | tf_op | source)
XLA Modules:
  0.0 142.6 jit_solution(17228252316700500597)
XLA Ops:
  0.0 138.2 %residual.1 = (f32[256,2304]{1,0:T(8,128)}, bf16[4,2304,384]{2,1,0:T(8,128)(2,1)}, bf16[4,384,1536]{2,1,0:T(8,128)(2,1)}) custom-call(s32[2,32]{1,0:T(2,128)} %bitcast.12, bf16[256,2304]{1,0:T(8,128)(2,1)} %bitcast.10, bf16[384,2304]{1,0:T(8,128)(2,1)} %bitcast.9, bf16[384,1536]{1,0:T(8,128)(2,1)} %bitcast.11), custom_call_target="tpu_custom_call" | custom-call | tf_op jit(solution)/shard_map/residual/pallas_call | solution.py:528
  138.2 4.4 %copy.5 = f32[16,16,2304]{2,1,0:T(8,128)} copy(f32[16,16,2304]{2,0,1:T(8,128)} %bitcast.8) | data formatting | bytes 4718592 | tf_op jit(solution)/shard_map/transpose | solution.py:577

commit v5 on v4

--- a/solution.py
+++ b/solution.py
@@ -72,7 +72,7 @@
     loop(DC // 4, body)
 
 
-PAIRS = 4
+PAIRS = 6
 
 
 def form(left, f, k, w):
@@ -403,11 +403,6 @@
     prepare(1)
     form_blocks(False, 2, 2)
     forward(2)
-    send_g(0)
-    send_g(1)
-    wait_diag(2)
-    prepare(2)
-    form_blocks(False, 4, SLOTS - 4)
     take_picked(0)
     swap_rows = one_hot(OO, O, O)
     flip_pairs(lw, swap_rows, plane, lall.at[at.own_slab])
@@ -416,6 +411,11 @@
     sent_picked(0)
 
     send_picked(1)
+    send_g(0)
+    send_g(1)
+    wait_diag(2)
+    prepare(2)
+    form_blocks(False, 4, SLOTS - 4)
     l_copy(0, at.mate_slab, at.mate).wait_recv()
     ladder_blocks(False, 0, SLOTS)
     form_blocks(False, SLOTS, last)

time: 143 us -> 140 us (0.979)
  Pallas kernels: 138 us -> 136 us
    pallas_call x1, Pallas kernels: 138 us -> 136 us  [call(): pl.pallas_call(functools.partial(kernel, n), out_shape=(jax.ShapeDtypeStr...]
where the time goes in v5:
time: 140 us
  Pallas kernels  136 us (97%)
  local copies, waits for them, and re-layouts  4.44 us (3%)
    pallas_call x1, Pallas kernels, call(): pl.pallas_call(functools.partial(kernel, n), out_shape=(jax.ShapeDtypeStr...  136 us
    transpose x1, local copies, waits for them, and re-layouts, local(): jnp.transpose(out.reshape(O, O, SLAB), (1, 0, 2)).reshape(1, OO, SLAB)  4.44 us

profile of v5, /device:TPU:1, one launch (start us, length us, event | category | flops | bytes accessed | tf_op | source)
XLA Modules:
  0.0 140.1 jit_solution(4667324390826447277)
XLA Ops:
  0.0 135.7 %residual.1 = (f32[256,2304]{1,0:T(8,128)}, bf16[4,2304,384]{2,1,0:T(8,128)(2,1)}, bf16[4,384,1536]{2,1,0:T(8,128)(2,1)}) custom-call(s32[2,32]{1,0:T(2,128)} %bitcast.12, bf16[256,2304]{1,0:T(8,128)(2,1)} %bitcast.10, bf16[384,2304]{1,0:T(8,128)(2,1)} %bitcast.9, bf16[384,1536]{1,0:T(8,128)(2,1)} %bitcast.11), custom_call_target="tpu_custom_call" | custom-call | tf_op jit(solution)/shard_map/residual/pallas_call | solution.py:528
  135.7 4.4 %copy.5 = f32[16,16,2304]{2,1,0:T(8,128)} copy(f32[16,16,2304]{2,0,1:T(8,128)} %bitcast.8) | data formatting | bytes 4718592 | tf_op jit(solution)/shard_map/transpose | solution.py:577
